TPU v7x, 32 devices: a whole 2x2x4 slice. The times are simulated.
32 devices in a mesh: dp: 8 (over y, x, core), fsdp: 4 (over z).
Axes of the slice: x: 2, y: 2, z: 4, core: 2. Of those that a mesh axis runs over, the one named last changes fastest.
Arguments:
- tokens: bfloat16 [38400, 768], P(('dp', 'fsdp')), may hold values from -6 to 6
- image_sides: int32 [64, 3], P(('dp', 'fsdp')), may hold values from 0 to 24, as said below
- out_grad: bfloat16 [38400, 768], P(('dp', 'fsdp')), may hold values from -6 to 6
- attn_norm: bfloat16 [2, 768], P(None, ('dp', 'fsdp'))
- qkv_weight: bfloat16 [768, 2304], P(('dp', 'fsdp')), may hold values from -0.21875 to 0.21875
- qkv_bias: bfloat16 [2304], P(('dp', 'fsdp')), may hold values from -4 to 4
- out_weight: bfloat16 [768, 768], P(('dp', 'fsdp')), may hold values from -1.75 to 1.75
- out_bias: bfloat16 [768], P(('dp', 'fsdp')), may hold values from -4 to 4
- frequencies: bfloat16 [768], P(('dp', 'fsdp')), may hold values from -1 to 1
- mlp_norm: bfloat16 [2, 768], P(None, ('dp', 'fsdp'))
- up_weight: bfloat16 [768, 3072], P(('dp', 'fsdp')), may hold values from -0.21875 to 0.21875
- up_bias: bfloat16 [3072], P(('dp', 'fsdp')), may hold values from -4 to 4
- down_weight: bfloat16 [3072, 768], P(None, ('dp', 'fsdp')), may hold values from -0.15625 to 0.15625
- down_bias: bfloat16 [768], P(('dp', 'fsdp')), may hold values from -4 to 4
Outputs:
- mixed_out: bfloat16 [38400, 768], P(('dp', 'fsdp'))
- token_grad: bfloat16 [38400, 768], P(('dp', 'fsdp'))
- attn_norm_grad: float32 [2, 768], P(None, ('dp', 'fsdp'))
- qkv_weight_grad: float32 [768, 2304], P(('dp', 'fsdp'))
- qkv_bias_grad: float32 [2304], P(('dp', 'fsdp'))
- out_weight_grad: float32 [768, 768], P(('dp', 'fsdp'))
- out_bias_grad: float32 [768], P(('dp', 'fsdp'))
- frequency_grad: float32 [768], P(('dp', 'fsdp'))
- mlp_norm_grad: float32 [2, 768], P(None, ('dp', 'fsdp'))
- up_weight_grad: float32 [768, 3072], P(('dp', 'fsdp'))
- up_bias_grad: float32 [3072], P(('dp', 'fsdp'))
- down_weight_grad: float32 [3072, 768], P(None, ('dp', 'fsdp'))
- down_bias_grad: float32 [768], P(('dp', 'fsdp'))
Inputs may be any that keep to these rules, and one draw needn't show every extreme that they name: `image_sides`: each row is one of (24, 0, 0), (20, 14, 0), (14, 20, 0), (14, 14, 14), (20, 0, 0), (14, 14, 0); the first row is (24, 0, 0).
All inputs are finite; a program needn't handle non-finite values.
Results may differ from a plain program's by a relative error of at most 0.012.
Values may be sent and summed in bfloat16 or wider, within the bound.
A program may use at most 256 MiB of HBM per device.

v0:
```python
import jax
import jax.numpy as jnp
from jax import lax
from jax.sharding import PartitionSpec as P

HEADS = 12
HD = 64


norm_eps = 1e-06
score_scale = 0.125


def layer_norm(values, gain_row, shift_row):
    average = jnp.mean(values, axis=-1, keepdims=True)
    centered = values - average
    variance = jnp.mean(centered * centered, axis=-1, keepdims=True)
    return centered * lax.rsqrt(variance + norm_eps) * gain_row + shift_row


def grid_places(sides, slot_rows):
    counts = sides * sides
    ends = jnp.cumsum(counts)
    row_index = jnp.arange(slot_rows, dtype=jnp.int32)
    segment = jnp.sum((row_index[:, None] >= ends[None, :]).astype(jnp.int32), axis=1)
    starts = jnp.concatenate([jnp.zeros((1,), jnp.int32), ends])
    widths = jnp.concatenate([sides, jnp.zeros((1,), jnp.int32)])
    picked = segment[:, None] == jnp.arange(4, dtype=jnp.int32)[None, :]
    start_row = jnp.sum(jnp.where(picked, starts[None, :], 0), axis=1)
    side_row = jnp.maximum(jnp.sum(jnp.where(picked, widths[None, :], 0), axis=1), 1)
    offset = row_index - start_row
    inside = segment < 3
    height = jnp.where(inside, offset // side_row, 0)
    across = jnp.where(inside, offset % side_row, 0)
    return (segment, height.astype(jnp.float32), across.astype(jnp.float32))


def rotate(query, key_part, frequency_values, height, across):
    table = frequency_values.reshape(2, HEADS, HD // 2)
    angle = height[:, None, None] * table[0][None] + across[:, None, None] * table[1][None]
    cosine = jnp.cos(angle)
    sine = jnp.sin(angle)

    def turn(part):
        part = part.reshape(part.shape[0], HEADS, HD)
        first_half = part[..., : HD // 2]
        second_half = part[..., HD // 2 :]
        return jnp.concatenate(
            [first_half * cosine - second_half * sine, first_half * sine + second_half * cosine],
            axis=-1,
        )

    return (turn(query), turn(key_part))


def left_product(first_arg, second_arg):
    return lax.dot_general(
        first_arg, second_arg, (((0,), (0,)), ((), ())), preferred_element_type=jnp.float32
    )


def right_product(first_arg, second_arg):
    return lax.dot_general(
        first_arg, second_arg, (((1,), (1,)), ((), ())), preferred_element_type=jnp.float32
    )


def forward_slot(slot_block, sides, attn_full, mlp_full):
    norm_one, w_qkv, b_qkv, w_out, b_out, frequency_full = attn_full
    norm_two, w_up, b_up, w_down, b_down = mlp_full
    slot_rows = slot_block.shape[0]
    model_width = w_out.shape[0]
    segment, height, across = grid_places(sides, slot_rows)
    start_value = slot_block.astype(jnp.float32)
    normed, norm_back = jax.vjp(
        layer_norm, start_value, norm_one[0].astype(jnp.float32), norm_one[1].astype(jnp.float32)
    )
    normed_low = normed.astype(jnp.bfloat16)
    mixed = jnp.dot(normed_low, w_qkv, preferred_element_type=jnp.float32) + b_qkv.astype(
        jnp.float32
    )

    def turn_both(query, key_part, frequency_values):
        return rotate(query, key_part, frequency_values, height, across)

    turned, rope_back = jax.vjp(
        turn_both,
        mixed[:, :model_width],
        mixed[:, model_width : 2 * model_width],
        frequency_full.astype(jnp.float32),
    )
    query_low = turned[0].astype(jnp.bfloat16)
    key_low = turned[1].astype(jnp.bfloat16)
    value_low = mixed[:, 2 * model_width :].astype(jnp.bfloat16).reshape(slot_rows, HEADS, HD)
    same_image = segment[:, None] == segment[None, :]
    scores = (
        jnp.einsum("qhd,khd->hqk", query_low, key_low, preferred_element_type=jnp.float32)
        * score_scale
    )
    scores = jnp.where(same_image[None], scores, -1e30)
    row_peak = jnp.max(scores, axis=-1, keepdims=True)
    weights = jnp.exp(scores - row_peak)
    row_total = jnp.sum(weights, axis=-1, keepdims=True)
    probabilities = (weights / row_total).astype(jnp.bfloat16)
    log_total = row_peak + jnp.log(row_total)
    attended = jnp.einsum(
        "hqk,khd->qhd", probabilities, value_low, preferred_element_type=jnp.float32
    )
    attended = attended.reshape(slot_rows, model_width).astype(jnp.bfloat16)
    middle = (
        start_value
        + jnp.dot(attended, w_out, preferred_element_type=jnp.float32)
        + b_out.astype(jnp.float32)
    )
    normed_two, norm_two_back = jax.vjp(
        layer_norm, middle, norm_two[0].astype(jnp.float32), norm_two[1].astype(jnp.float32)
    )
    normed_two_low = normed_two.astype(jnp.bfloat16)
    hidden = jnp.dot(normed_two_low, w_up, preferred_element_type=jnp.float32) + b_up.astype(
        jnp.float32
    )
    activated, gelu_back = jax.vjp(jax.nn.gelu, hidden)
    activated_low = activated.astype(jnp.bfloat16)
    result = jnp.dot(activated_low, w_down, preferred_element_type=jnp.float32) + b_down.astype(
        jnp.float32
    )
    output = (middle + result).astype(jnp.bfloat16)
    saved = (
        norm_back,
        normed_low,
        rope_back,
        query_low,
        key_low,
        value_low,
        same_image,
        log_total,
        attended,
        norm_two_back,
        normed_two_low,
        gelu_back,
        activated_low,
    )
    return (output, saved)


def backward_slot(saved, grad_block, attn_full, mlp_full):
    (
        norm_back,
        normed_low,
        rope_back,
        query_low,
        key_low,
        value_low,
        same_image,
        log_total,
        attended,
        norm_two_back,
        normed_two_low,
        gelu_back,
        activated_low,
    ) = saved
    norm_one, w_qkv, b_qkv, w_out, b_out, frequency_full = attn_full
    norm_two, w_up, b_up, w_down, b_down = mlp_full
    slot_rows = grad_block.shape[0]
    model_width = w_out.shape[0]
    grad_value = grad_block.astype(jnp.float32)
    down_grad = left_product(activated_low, grad_block)
    down_bias_grad = jnp.sum(grad_value, axis=0)
    (hidden_grad,) = gelu_back(right_product(grad_block, w_down))
    hidden_low = hidden_grad.astype(jnp.bfloat16)
    up_grad = left_product(normed_two_low, hidden_low)
    up_bias_grad = jnp.sum(hidden_low.astype(jnp.float32), axis=0)
    middle_part, gain_two, shift_two = norm_two_back(right_product(hidden_low, w_up))
    middle_grad = grad_value + middle_part
    middle_low = middle_grad.astype(jnp.bfloat16)
    out_grad_weight = left_product(attended, middle_low)
    out_grad_bias = jnp.sum(middle_low.astype(jnp.float32), axis=0)
    attended_grad = (
        right_product(middle_low, w_out).astype(jnp.bfloat16).reshape(slot_rows, HEADS, HD)
    )
    scores = (
        jnp.einsum("qhd,khd->hqk", query_low, key_low, preferred_element_type=jnp.float32)
        * score_scale
    )
    scores = jnp.where(same_image[None], scores, -1e30)
    full_probs = jnp.exp(scores - log_total)
    probs_low = full_probs.astype(jnp.bfloat16)
    probability_grad = jnp.einsum(
        "qhd,khd->hqk", attended_grad, value_low, preferred_element_type=jnp.float32
    )
    value_grad = jnp.einsum(
        "hqk,qhd->khd", probs_low, attended_grad, preferred_element_type=jnp.float32
    )
    row_inner = jnp.sum(full_probs * probability_grad, axis=-1, keepdims=True)
    score_low = (full_probs * (probability_grad - row_inner)).astype(jnp.bfloat16)
    query_grad = (
        jnp.einsum("hqk,khd->qhd", score_low, key_low, preferred_element_type=jnp.float32)
        * score_scale
    )
    key_grad = (
        jnp.einsum("hqk,qhd->khd", score_low, query_low, preferred_element_type=jnp.float32)
        * score_scale
    )
    query_pre, key_pre, frequency_grad = rope_back((query_grad, key_grad))
    mixed_grad = jnp.concatenate(
        [query_pre, key_pre, value_grad.reshape(slot_rows, model_width)], axis=1
    ).astype(jnp.bfloat16)
    qkv_grad = left_product(normed_low, mixed_grad)
    qkv_bias_sum = jnp.sum(mixed_grad.astype(jnp.float32), axis=0)
    start_part, gain_one, shift_one = norm_back(right_product(mixed_grad, w_qkv))
    block_grad = (middle_grad + start_part).astype(jnp.bfloat16)
    attn_terms = (
        jnp.stack([gain_one, shift_one]),
        qkv_grad,
        qkv_bias_sum,
        out_grad_weight,
        out_grad_bias,
        frequency_grad,
    )
    mlp_terms = (jnp.stack([gain_two, shift_two]), up_grad, up_bias_grad, down_grad, down_bias_grad)
    return (block_grad, attn_terms, mlp_terms)


def on_device(
    tokens,
    image_sides,
    out_grad,
    attn_norm,
    qkv_weight,
    qkv_bias,
    out_weight,
    out_bias,
    frequencies,
    mlp_norm,
    up_weight,
    up_bias,
    down_weight,
    down_bias,
):
    micro_count = image_sides.shape[0]
    slot_rows = tokens.shape[0] // micro_count
    attn_full = (
        lax.all_gather(attn_norm, ("dp", "fsdp"), axis=1, tiled=True),
        lax.all_gather(qkv_weight, ("dp", "fsdp"), axis=0, tiled=True),
        lax.all_gather(qkv_bias, ("dp", "fsdp"), axis=0, tiled=True),
        lax.all_gather(out_weight, ("dp", "fsdp"), axis=0, tiled=True),
        lax.all_gather(out_bias, ("dp", "fsdp"), axis=0, tiled=True),
        lax.all_gather(frequencies, ("dp", "fsdp"), axis=0, tiled=True),
    )
    mlp_full = (
        lax.all_gather(mlp_norm, ("dp", "fsdp"), axis=1, tiled=True),
        lax.all_gather(up_weight, ("dp", "fsdp"), axis=0, tiled=True),
        lax.all_gather(up_bias, ("dp", "fsdp"), axis=0, tiled=True),
        lax.all_gather(down_weight, ("dp", "fsdp"), axis=1, tiled=True),
        lax.all_gather(down_bias, ("dp", "fsdp"), axis=0, tiled=True),
    )
    outputs = []
    saved_list = []
    for slot_index in range(micro_count):
        slot_block = tokens[slot_index * slot_rows : (slot_index + 1) * slot_rows]
        output, saved = forward_slot(slot_block, image_sides[slot_index], attn_full, mlp_full)
        outputs.append(output)
        saved_list.append(saved)
    attn_back = (
        lax.all_gather(attn_norm, ("dp", "fsdp"), axis=1, tiled=True),
        lax.all_gather(qkv_weight, ("dp", "fsdp"), axis=0, tiled=True),
        lax.all_gather(qkv_bias, ("dp", "fsdp"), axis=0, tiled=True),
        lax.all_gather(out_weight, ("dp", "fsdp"), axis=0, tiled=True),
        lax.all_gather(out_bias, ("dp", "fsdp"), axis=0, tiled=True),
        lax.all_gather(frequencies, ("dp", "fsdp"), axis=0, tiled=True),
    )
    mlp_back = (
        lax.all_gather(mlp_norm, ("dp", "fsdp"), axis=1, tiled=True),
        lax.all_gather(up_weight, ("dp", "fsdp"), axis=0, tiled=True),
        lax.all_gather(up_bias, ("dp", "fsdp"), axis=0, tiled=True),
        lax.all_gather(down_weight, ("dp", "fsdp"), axis=1, tiled=True),
        lax.all_gather(down_bias, ("dp", "fsdp"), axis=0, tiled=True),
    )
    block_grads = []
    attn_total = None
    mlp_total = None
    for slot_index in range(micro_count):
        grad_block = out_grad[slot_index * slot_rows : (slot_index + 1) * slot_rows]
        block_grad, attn_terms, mlp_terms = backward_slot(
            saved_list[slot_index], grad_block, attn_back, mlp_back
        )
        block_grads.append(block_grad)
        if attn_total is None:
            attn_total = attn_terms
            mlp_total = mlp_terms
        else:
            attn_total = jax.tree.map(jnp.add, attn_total, attn_terms)
            mlp_total = jax.tree.map(jnp.add, mlp_total, mlp_terms)
    attn_sums = (
        lax.psum_scatter(attn_total[0], ("dp", "fsdp"), scatter_dimension=1, tiled=True),
        lax.psum_scatter(attn_total[1], ("dp", "fsdp"), scatter_dimension=0, tiled=True),
        lax.psum_scatter(attn_total[2], ("dp", "fsdp"), scatter_dimension=0, tiled=True),
        lax.psum_scatter(attn_total[3], ("dp", "fsdp"), scatter_dimension=0, tiled=True),
        lax.psum_scatter(attn_total[4], ("dp", "fsdp"), scatter_dimension=0, tiled=True),
        lax.psum_scatter(attn_total[5], ("dp", "fsdp"), scatter_dimension=0, tiled=True),
    )
    mlp_sums = (
        lax.psum_scatter(mlp_total[0], ("dp", "fsdp"), scatter_dimension=1, tiled=True),
        lax.psum_scatter(mlp_total[1], ("dp", "fsdp"), scatter_dimension=0, tiled=True),
        lax.psum_scatter(mlp_total[2], ("dp", "fsdp"), scatter_dimension=0, tiled=True),
        lax.psum_scatter(mlp_total[3], ("dp", "fsdp"), scatter_dimension=1, tiled=True),
        lax.psum_scatter(mlp_total[4], ("dp", "fsdp"), scatter_dimension=0, tiled=True),
    )
    mixed_out = jnp.concatenate(outputs, axis=0)
    token_grad = jnp.concatenate(block_grads, axis=0)
    return (
        mixed_out,
        token_grad,
        attn_sums[0],
        attn_sums[1],
        attn_sums[2],
        attn_sums[3],
        attn_sums[4],
        attn_sums[5],
        mlp_sums[0],
        mlp_sums[1],
        mlp_sums[2],
        mlp_sums[3],
        mlp_sums[4],
    )


def solution(mesh):
    in_specs = (
        P(("dp", "fsdp"), None),
        P(("dp", "fsdp"), None),
        P(("dp", "fsdp"), None),
        P(None, ("dp", "fsdp")),
        P(("dp", "fsdp"), None),
        P(("dp", "fsdp")),
        P(("dp", "fsdp"), None),
        P(("dp", "fsdp")),
        P(("dp", "fsdp")),
        P(None, ("dp", "fsdp")),
        P(("dp", "fsdp"), None),
        P(("dp", "fsdp")),
        P(None, ("dp", "fsdp")),
        P(("dp", "fsdp")),
    )
    out_specs = (
        P(("dp", "fsdp"), None),
        P(("dp", "fsdp"), None),
        P(None, ("dp", "fsdp")),
        P(("dp", "fsdp"), None),
        P(("dp", "fsdp")),
        P(("dp", "fsdp"), None),
        P(("dp", "fsdp")),
        P(("dp", "fsdp")),
        P(None, ("dp", "fsdp")),
        P(("dp", "fsdp"), None),
        P(("dp", "fsdp")),
        P(None, ("dp", "fsdp")),
        P(("dp", "fsdp")),
    )
    return jax.shard_map(
        on_device, mesh=mesh, in_specs=in_specs, out_specs=out_specs, check_vma=False
    )
```

profile of v0, /device:TPU:0, one launch (start us, length us, event | category | flops | bytes accessed | tf_op | source)
XLA Modules:
  0.0 934.7 jit_solution(18159715088897972748)
XLA Ops:
  15.6 42.7 %all-reduce.25 = (bf16[2304]{0:T(1024)(128)(2,1)S(1)}, bf16[768]{0:T(1024)(128)(2,1)S(1)}, bf16[768]{0:T(1024)(128)(2,1)S(1)}, bf16[768]{0:T(1024)(128)(2,1)}, bf16[3072]{0:T(1024)(128)(2,1)S(1)}) all-reduce(bf16[2304]{0:T(1024)(128)(2,1)S(1)} %dynamic-update-slice, ...), channel_id=1, replica_groups=mesh['dp'=8,'fsdp'=4] {'dp','fsdp'}, use_global_device_ids=true, to_apply=%add.12 | all-reduce | flops 7680 | bytes 30720
  63.8 65.4 %all-gather = bf16[32,24,2]{1,2,0:T(2,128)(2,1)S(1)} all-gather(bf16[1,24,2]{1,2,0:T(2,128)(2,1)S(1)} %bitcast.148), channel_id=1, replica_groups=mesh['dp'=8,'fsdp'=4] {'dp','fsdp'}, dimensions={0}, use_global_device_ids=true | all-gather | bytes 3168 | tf_op jit(solution)/shard_map/all_gather | solution.py:243
  129.4 63.2 %all-gather.1 = bf16[32,24,2]{1,2,0:T(2,128)(2,1)S(1)} all-gather(bf16[1,24,2]{1,2,0:T(2,128)(2,1)S(1)} %bitcast.149), channel_id=1, replica_groups=mesh['dp'=8,'fsdp'=4] {'dp','fsdp'}, dimensions={0}, use_global_device_ids=true | all-gather | bytes 3168 | tf_op jit(solution)/shard_map/all_gather | solution.py:251
  208.4 6.6 subtract_convert_fusion.3
  215.1 8.3 fusion.120
  223.4 8.9 fusion
  232.3 10.9 %fusion.51 = bf16[12,64,600]{2,1,0:T(8,128)(2,1)} fusion(bf16[600,12,64]{0,2,1:T(8,128)(2,1)S(1)} %bitcast.126, f32[12,600,600]{1,2,0:T(8,128)} %get-tuple-element.125, f32[12,600]{1,0:T(8,128)S(1)} %fusion, f32[12,600]{1,0:T(8,128)S(1)} %get-tuple-element.124), kind=kOutput, calls=%fused_computation.119 | convolution fusion | flops 566380800 | bytes 19180800 | tf_op jit(solution)/shard_map/hqk,khd->qhd/dot_general | solution.py:106
  269.5 8.1 fusion.118
  277.7 8.8 fusion.1
  286.5 9.9 %fusion.50 = bf16[12,64,600]{2,1,0:T(8,128)(2,1)S(1)} fusion(bf16[600,12,64]{0,2,1:T(8,128)(2,1)S(1)} %bitcast.128, f32[12,600,600]{1,2,0:T(8,128)} %get-tuple-element.121, f32[12,600]{1,0:T(8,128)S(1)} %fusion.1, f32[12,600]{1,0:T(8,128)S(1)} %get-tuple-element.120), kind=kOutput, calls=%fused_computation.118 | convolution fusion | flops 566380800 | bytes 19180800 | tf_op jit(solution)/shard_map/hqk,khd->qhd/dot_general | solution.py:106
  299.1 9.2 fusion.109
  313.9 12.7 %convert_reduce_fusion.1 = (f32[3072]{0:T(1024)}, bf16[600,3072]{1,0:T(8,128)(2,1)S(1)}) fusion(f32[600,3072]{1,0:T(8,128)} %fusion.109, f32[3072]{0:T(1024)S(1)} %convert_element_type.201, bf16[3072,768]{0,1:T(8,128)(2,1)} %all-gather.13.cloned.1.call-done, bf16[1200,768]{1,0:T(8,128)(2,1)} %param.16), kind=kOutput, calls=%fused_computation.41 | convolution fusion | flops 2873545728 | bytes 16723968 | tf_op jit(solution)/shard_map/dot_general | solution.py:63
  326.5 8.4 convert_reduce_fusion
  350.3 11.8 %multiply_reduce_fusion.1 = (f32[12,600]{1,0:T(8,128)S(1)}, f32[12,600,600]{1,2,0:T(8,128)}) fusion(f32[12,600,600]{1,2,0:T(8,128)} %get-tuple-element.125, f32[12,600]{1,0:T(8,128)S(1)} %log_add_fusion.1, bf16[600,12,64]{0,2,1:T(8,128)(2,1)S(1)} %bitcast.110, bf16[600,12,64]{0,2,1:T(8,128)(2,1)S(1)} %bitcast.127), kind=kOutput, calls=%fused_computation.4 | convolution fusion | flops 565912832 | bytes 36460800 | tf_op jit(solution)/shard_map/qhd,khd->hqk/dot_general | solution.py:188
  362.0 13.4 %multiply_convert_fusion.1 = bf16[12,600,600]{1,2,0:T(8,128)(2,1)S(1)} fusion(f32[12,600,600]{1,2,0:T(8,128)} %get-tuple-element.132, f32[12,600,600]{1,2,0:T(8,128)} %get-tuple-element.125, f32[12,600]{1,0:T(8,128)S(1)} %get-tuple-element.131, f32[12,600]{1,0:T(8,128)S(1)} %log_add_fusion.1), kind=kLoop, calls=%fused_computation.3 | loop fusion | flops 17280000 | bytes 43257600 | tf_op jit(solution)/shard_map/convert_element_type | solution.py:195
  386.2 12.1 %multiply_reduce_fusion = (f32[12,600]{1,0:T(8,128)S(1)}, f32[12,600,600]{1,2,0:T(8,128)}) fusion(f32[12,600,600]{1,2,0:T(8,128)} %get-tuple-element.121, f32[12,600]{1,0:T(8,128)S(1)} %log_add_fusion, bf16[600,12,64]{0,2,1:T(8,128)(2,1)S(1)} %bitcast.112, bf16[600,12,64]{0,2,1:T(8,128)(2,1)S(1)} %bitcast.129), kind=kOutput, calls=%fused_computation.1 | convolution fusion | flops 565912832 | bytes 36460800 | tf_op jit(solution)/shard_map/qhd,khd->hqk/dot_general | solution.py:188
  398.2 13.0 %multiply_convert_fusion = bf16[12,600,600]{1,2,0:T(8,128)(2,1)S(1)} fusion(f32[12,600,600]{1,2,0:T(8,128)} %get-tuple-element.130, f32[12,600,600]{1,2,0:T(8,128)} %get-tuple-element.121, f32[12,600]{1,0:T(8,128)S(1)} %get-tuple-element.129, f32[12,600]{1,0:T(8,128)S(1)} %log_add_fusion), kind=kLoop, calls=%fused_computation | loop fusion | flops 17280000 | bytes 43257600 | tf_op jit(solution)/shard_map/convert_element_type | solution.py:195
  422.5 7.6 multiply_add_fusion.1
  436.9 7.7 multiply_reduce_fusion.9
  445.1 10.2 %fusion.52 = bf16[12,64,600]{2,1,0:T(8,128)(2,1)S(1)} fusion(bf16[600,12,64]{0,2,1:T(8,128)(2,1)S(1)} %bitcast.111, f32[12,600,600]{1,2,0:T(8,128)} %get-tuple-element.125, f32[12,600]{1,0:T(8,128)S(1)} %log_add_fusion.1), kind=kOutput, calls=%fused_computation.120 | convolution fusion | flops 562060800 | bytes 19152000 | tf_op jit(solution)/shard_map/hqk,qhd->khd/dot_general | solution.py:191
  461.7 9.1 fusion.55
  471.8 9.9 %convolution_add_fusion = f32[768,2304]{1,0:T(8,128)} fusion(f32[768,2304]{1,0:T(8,128)} %fusion.99, f32[600]{0:T(1024)S(1)} %copy-done.102, f32[600]{0:T(1024)S(1)} %copy-done.86, f32[768]{0:T(1024)S(1)} %copy-done.110, f32[768]{0:T(1024)S(1)} %copy-done.98, bf16[1200,768]{1,0:T(8,128)(2,1)S(1)} %copy-done.1, bf16[600,768]{0,1:T(8,128)(2,1)S(1)} %bitcast.133, ...), kind=kOutput, calls=%fused_computation.46 | convolution fusion | flops 2136195072 | bytes 18042880 | tf_op jit(solution)/shard_map/dot_general | solution.py:57
  481.7 8.1 fusion.69
  489.8 11.4 %convolution_add_fusion.1 = f32[3072,768]{0,1:T(8,128)} fusion(f32[3072,768]{0,1:T(8,128)S(1)} %fusion.69, bf16[1200,768]{1,0:T(8,128)(2,1)S(1)} %copy-done.23, f32[600,3072]{1,0:T(8,128)} %fusion.110, f32[3072]{0:T(1024)S(1)} %convert_element_type.201), kind=kOutput, calls=%fused_computation.47 | convolution fusion | flops 2851946496 | bytes 27181056 | tf_op jit(solution)/shard_map/dot_general | solution.py:57
  501.9 7.0 fusion.108
  508.9 7.4 convolution_add_fusion.2
  530.3 40.9 %all-reduce.24 = (f32[2,768]{1,0:T(2,128)S(1)}, f32[2304]{0:T(1024)S(1)}, f32[768]{0:T(1024)S(1)}, f32[768]{0:T(1024)S(1)}, f32[2,768]{1,0:T(2,128)S(1)}, /*index=5*/f32[3072]{0:T(1024)S(1)}, f32[768]{0:T(1024)S(1)}) all-reduce(f32[2,768]{1,0:T(2,128)S(1)} %maximum_add_fusion, ...), channel_id=2, replica_groups=mesh['dp'=8,'fsdp'=4] {'dp','fsdp'}, use_global_device_ids=true, to_apply=%region_34.35.clone | all-reduce | flops 10752 | bytes 86016
  575.4 10.8 %add_convert_fusion.8 = bf16[600,768]{1,0:T(8,128)(2,1)S(1)} fusion(f32[600,768]{1,0:T(8,128)} %copy-done.13, bf16[3072,768]{0,1:T(8,128)(2,1)} %all-gather.13.cloned.1.call-done, f32[768]{0:T(1024)S(1)} %convert_element_type.203, f32[600,3072]{1,0:T(8,128)} %fusion.109, f32[3072]{0:T(1024)S(1)} %convert_element_type.201), kind=kOutput, calls=%fused_computation.114 | convolution fusion | flops 2850969600 | bytes 14871552 | tf_op jit(solution)/shard_map/dot_general | solution.py:124
  586.3 9.3 add_convert_fusion.6
  601.6 42.6 %reduce-scatter.7.cloned.1.call-done = f32[24,2304]{1,0:T(8,128)} async-done(((f32[768,2304]{1,0:T(8,128)}), f32[24,2304]{1,0:T(8,128)}) %reduce-scatter.7.cloned.1.call-update) | async-done | bytes 221200 | tf_op jit(solution)/shard_map/reduce_scatter | solution.py:296
  644.2 141.4 %reduce-scatter.13.cloned.1.call-done = f32[3072,24]{0,1:T(8,128)} async-done(((f32[3072,768]{0,1:T(8,128)}), f32[3072,24]{0,1:T(8,128)}) %reduce-scatter.13.cloned.1.call-update) | async-done | bytes 294928 | tf_op jit(solution)/shard_map/reduce_scatter | solution.py:306
  785.5 142.2 %reduce-scatter.11.cloned.1.call-done = f32[24,3072]{1,0:T(8,128)} async-done(((f32[768,3072]{1,0:T(8,128)}), f32[24,3072]{1,0:T(8,128)}) %reduce-scatter.11.cloned.1.call-update) | async-done | bytes 294928 | tf_op jit(solution)/shard_map/reduce_scatter | solution.py:304
  (406 shorter events, 140.0 us)
Async XLA Ops:
  7.2 55.3 %copy-start = (bf16[1200,768]{1,0:T(8,128)(2,1)S(1)}, bf16[1200,768]{1,0:T(8,128)(2,1)}, u32[]{:S(2)}) copy-start(bf16[1200,768]{1,0:T(8,128)(2,1)} %param.14) | copy-start | bytes 5529604
  7.2 185.5 %all-gather.7.cloned.1.call-start = ((), (), s32[]{:S(2)}) async-start(), calls=%async_computation.4 | async-start | bytes 3649536 | tf_op jit(solution)/shard_map/all_gather | solution.py:244
  7.9 253.6 %all-gather.9.cloned.1.call-start = ((), (), s32[]{:S(2)}) async-start(), calls=%async_computation.5 | async-start | bytes 1216512 | tf_op jit(solution)/shard_map/all_gather | solution.py:246
  8.7 290.4 %all-gather.11.cloned.1.call-start = ((), (), s32[]{:S(2)}) async-start(), calls=%async_computation.6 | async-start | bytes 4866048 | tf_op jit(solution)/shard_map/all_gather | solution.py:252
  9.4 304.4 %all-gather.13.cloned.1.call-start = ((), (), s32[]{:S(2)}) async-start(), calls=%async_computation.7 | async-start | bytes 4866048 | tf_op jit(solution)/shard_map/all_gather | solution.py:254
  10.0 591.6 %reduce-scatter.9.cloned.1.call-start = ((), (), s32[]{:S(2)}) async-start(), calls=%async_computation.9 | async-start | bytes 2433024 | tf_op jit(solution)/shard_map/reduce_scatter | solution.py:298
  58.4 206.3 %copy-start.73 = (f32[12,32]{1,0:T(8,128)}, f32[12,32]{1,0:T(8,128)S(1)}, u32[]{:S(2)}) copy-start(f32[12,32]{1,0:T(8,128)S(1)} %slice.116) | copy-start | bytes 4612
  58.4 71.0 %copy-start.117 = (bf16[2,24]{1,0:T(2,128)(2,1)S(1)}, bf16[2,24]{1,0:T(2,128)(2,1)}, u32[]{:S(2)}) copy-start(bf16[2,24]{1,0:T(2,128)(2,1)} %param.23) | copy-start | bytes 292
  59.0 205.7 %copy-start.77 = (f32[600]{0:T(1024)}, f32[600]{0:T(1024)S(1)}, u32[]{:S(2)}) copy-start(f32[600]{0:T(1024)S(1)} %get-tuple-element.69) | copy-start | bytes 7204
  59.1 205.6 %copy-start.81 = (f32[600]{0:T(1024)}, f32[600]{0:T(1024)S(1)}, u32[]{:S(2)}) copy-start(f32[600]{0:T(1024)S(1)} %fusion.82) | copy-start | bytes 7204
  60.4 148.0 %copy-start.79 = (f32[600]{0:T(1024)}, f32[600]{0:T(1024)S(1)}, u32[]{:S(2)}) copy-start(f32[600]{0:T(1024)S(1)} %get-tuple-element.67) | copy-start | bytes 7204
  60.5 147.9 %copy-start.83 = (f32[600]{0:T(1024)}, f32[600]{0:T(1024)S(1)}, u32[]{:S(2)}) copy-start(f32[600]{0:T(1024)S(1)} %fusion.78) | copy-start | bytes 7204
  60.6 204.1 %copy-start.75 = (f32[12,32]{1,0:T(8,128)}, f32[12,32]{1,0:T(8,128)S(1)}, u32[]{:S(2)}) copy-start(f32[12,32]{1,0:T(8,128)S(1)} %slice.118) | copy-start | bytes 4612
  62.4 135.0 %copy-start.87 = (f32[600]{0:T(1024)}, f32[600]{0:T(1024)S(1)}, u32[]{:S(2)}) copy-start(f32[600]{0:T(1024)S(1)} %get-tuple-element.139) | copy-start | bytes 7204
  62.4 180.7 %copy-start.85 = (f32[600]{0:T(1024)}, f32[600]{0:T(1024)S(1)}, u32[]{:S(2)}) copy-start(f32[600]{0:T(1024)S(1)} %get-tuple-element.138) | copy-start | bytes 7204
  63.2 134.2 %copy-start.99 = (f32[600]{0:T(1024)}, f32[600]{0:T(1024)S(1)}, u32[]{:S(2)}) copy-start(f32[600]{0:T(1024)S(1)} %fusion.85) | copy-start | bytes 7204
  63.2 180.0 %copy-start.101 = (f32[600]{0:T(1024)}, f32[600]{0:T(1024)S(1)}, u32[]{:S(2)}) copy-start(f32[600]{0:T(1024)S(1)} %fusion.87) | copy-start | bytes 7204
  129.3 113.9 %copy-start.97 = (f32[768]{0:T(1024)}, f32[768]{0:T(1024)S(1)}, u32[]{:S(2)}) copy-start(f32[768]{0:T(1024)S(1)} %get-tuple-element.45) | copy-start | bytes 9220
  129.3 113.9 %copy-start.109 = (f32[768]{0:T(1024)}, f32[768]{0:T(1024)S(1)}, u32[]{:S(2)}) copy-start(f32[768]{0:T(1024)S(1)} %get-tuple-element.46) | copy-start | bytes 9220
  192.7 115.6 %copy-start.70 = (f32[768]{0:T(1024)}, f32[768]{0:T(1024)S(1)}, u32[]{:S(2)}) copy-start(f32[768]{0:T(1024)S(1)} %get-tuple-element.44) | copy-start | bytes 9220
  202.3 29.9 %copy-start.37 = (bf16[600,768]{0,1:T(8,128)(2,1)}, bf16[600,768]{0,1:T(8,128)(2,1)S(1)}, u32[]{:S(2)}) copy-start(bf16[600,768]{0,1:T(8,128)(2,1)S(1)} %copy.88) | copy-start | bytes 2764804
  250.8 35.7 %copy-start.39 = (bf16[600,768]{0,1:T(8,128)(2,1)}, bf16[600,768]{0,1:T(8,128)(2,1)S(1)}, u32[]{:S(2)}) copy-start(bf16[600,768]{0,1:T(8,128)(2,1)S(1)} %copy.93) | copy-start | bytes 2764804
  313.9 21.1 %slice-start = ((s8[4718592]{0:T(1024)(128)(4,1)}), s8[4194304]{0:T(1024)(128)(4,1)S(1)}, s32[]{:S(2)}) async-start(s8[4718592]{0:T(1024)(128)(4,1)} %bitcast.150), calls=%async_computation.12 | async-start | bytes 8388608
  362.0 13.4 %copy-start.53 = (bf16[600,12,32]{0,2,1:T(8,128)(2,1)S(1)}, bf16[600,12,32]{0,2,1:T(8,128)(2,1)}, u32[]{:S(2)}) copy-start(bf16[600,12,32]{0,2,1:T(8,128)(2,1)} %copy-done.52) | copy-start | bytes 1382404
  362.0 13.4 %copy-start.55 = (bf16[600,12,32]{0,2,1:T(8,128)(2,1)S(1)}, bf16[600,12,32]{0,2,1:T(8,128)(2,1)}, u32[]{:S(2)}) copy-start(bf16[600,12,32]{0,2,1:T(8,128)(2,1)} %copy-done.54) | copy-start | bytes 1382404
  398.2 13.0 %copy-start.59 = (bf16[600,12,32]{0,2,1:T(8,128)(2,1)S(1)}, bf16[600,12,32]{0,2,1:T(8,128)(2,1)}, u32[]{:S(2)}) copy-start(bf16[600,12,32]{0,2,1:T(8,128)(2,1)} %copy-done.58) | copy-start | bytes 1382404
  421.0 223.2 %reduce-scatter.7.cloned.1.call-start = ((), (), s32[]{:S(2)}) async-start(), calls=%async_computation.8 | async-start | bytes 7299072 | tf_op jit(solution)/shard_map/reduce_scatter | solution.py:296
  431.7 23.6 %copy-start.29 = (bf16[600,12,64]{0,2,1:T(8,128)(2,1)}, bf16[600,12,64]{0,2,1:T(8,128)(2,1)S(1)}, u32[]{:S(2)}) copy-start(bf16[600,12,64]{0,2,1:T(8,128)(2,1)S(1)} %add_convert_fusion.3) | copy-start | bytes 2764804
  444.8 26.1 %copy-start.31 = (bf16[600,12,64]{0,2,1:T(8,128)(2,1)}, bf16[600,12,64]{0,2,1:T(8,128)(2,1)S(1)}, u32[]{:S(2)}) copy-start(bf16[600,12,64]{0,2,1:T(8,128)(2,1)S(1)} %add_convert_fusion) | copy-start | bytes 2764804
  445.1 25.8 %copy-start.35 = (bf16[600,12,64]{0,2,1:T(8,128)(2,1)}, bf16[600,12,64]{0,2,1:T(8,128)(2,1)S(1)}, u32[]{:S(2)}) copy-start(bf16[600,12,64]{0,2,1:T(8,128)(2,1)S(1)} %add_convert_fusion.1) | copy-start | bytes 2764804
  481.7 303.9 %reduce-scatter.13.cloned.1.call-start = ((), (), s32[]{:S(2)}) async-start(), calls=%async_computation.11 | async-start | bytes 9732096 | tf_op jit(solution)/shard_map/reduce_scatter | solution.py:306
  501.2 426.5 %reduce-scatter.11.cloned.1.call-start = ((), (), s32[]{:S(2)}) async-start(), calls=%async_computation.10 | async-start | bytes 9732096 | tf_op jit(solution)/shard_map/reduce_scatter | solution.py:304
  (105 other events, 557.6 us)
Sparse Core Ops, SparseCore 0:
  10.8 62.9 all-gather.6
  76.6 52.8 all-gather.8
  132.3 62.6 all-gather.10
  197.6 62.4 all-gather.12
  421.1 97.8 reduce-scatter.8
  526.1 118.0 reduce-scatter.6
  650.7 134.8 reduce-scatter.12
  793.0 134.6 reduce-scatter.10
where the time goes:
time: 941 us; the launch traced here: 935 us
  waiting for transfers between devices  329 us (35%)
  matrix products  235 us (25%)
  blocking collectives  212 us (23%)
  other arithmetic  94.4 us (10%)
  local copies, waits for them, and re-layouts  47.5 us (5%)
  between operations  16.2 us (2%)
    reduce_scatter x1, waiting for transfers between devices, on_device(): lax.psum_scatter(mlp_total[1], ('dp', 'fsdp'), scatter_dimension=0, tiled...  142 us
    reduce_scatter x1, waiting for transfers between devices, on_device(): lax.psum_scatter(mlp_total[3], ('dp', 'fsdp'), scatter_dimension=1, tiled...  141 us
    unnamed x2, blocking collectives  83.6 us
    all_gather x1, blocking collectives, on_device(): lax.all_gather(attn_norm, ('dp', 'fsdp'), axis=1, tiled=True)  65.4 us
    all_gather x1, blocking collectives, on_device(): lax.all_gather(mlp_norm, ('dp', 'fsdp'), axis=1, tiled=True)  63.2 us
    dot_general x8, matrix products, left_product(): lax.dot_general(first_arg, second_arg, (((0,), (0,)), ((), ())), preferre...  55 us
    reduce_scatter x1, waiting for transfers between devices, on_device(): lax.psum_scatter(attn_total[1], ('dp', 'fsdp'), scatter_dimension=0, tile...  42.6 us
    dot_general x8, matrix products, right_product(): lax.dot_general(first_arg, second_arg, (((1,), (1,)), ((), ())), preferre...  39.8 us
  transfers between devices with their start and end apart: 8, of which 3 were waited for; matrix products, arithmetic and copies ran while one was open for 28% of the time, Pallas kernels for 0%

commit v1 on v0

v1 whole, which is shorter than its diff:
```python
import functools
import jax
import jax.numpy as jnp
from jax import lax
from jax.experimental import pallas as pl
from jax.experimental.pallas import tpu as pltpu
from jax.sharding import PartitionSpec as P

HEADS = 12
HD = 64
HALF = HD // 2
GROUP = 4
GROUPS = HEADS // GROUP
GW = GROUP * HD
CHUNK = 512
FIRST = 3
EARLY = 3
PLACES = 32
EPS = 1e-06
SCALE = 0.125
GELU_A = 0.7978845608028654
GELU_B = GELU_A * 0.044715
MASKED = -1e30
LANES = 128
BOTH = ("dp", "fsdp")
F32 = jnp.float32
BF16 = jnp.bfloat16
ANY = pl.BlockSpec(memory_space=pl.ANY)
SD = jax.ShapeDtypeStruct


def dot(a, b, ca, cb):
    return lax.dot_general(a, b, (((ca,), (cb,)), ((), ())), preferred_element_type=F32)


class Grid:
    def __init__(self, dp, fsdp):
        self.P, self.Z = dp // 2, fsdp
        i = lax.axis_index("dp")
        self.core, self.z = i % 2, lax.axis_index("fsdp")
        self.ring = self.turn(i // 2)

    def turn(self, p):
        return p + (p // 2) * (5 - 2 * p)

    def place(self, d):
        return self.turn((self.ring + d + self.P) % self.P)

    def at(self, d=0, core=None, k=0):
        core = self.core if core is None else core
        return (self.place(d) * 2 + core, (self.z + k + self.Z) % self.Z)

    def block(self, d=0, k=0):
        a, b = self.at(d, None, k)
        return self.place(d), self.core, b

    def line(self, d=0):
        return self.place(d), self.core

    def sibling(self):
        return self.at(core=1 - self.core)


def greet(g):
    barrier = pltpu.get_barrier_semaphore()
    for w in [g.at(1), g.at(-1), g.sibling()] + [g.at(k=k) for k in range(1, g.Z)]:
        pl.semaphore_signal(barrier, inc=1, device_id=w, device_id_type=pl.DeviceIdType.MESH)


def met(g):
    pl.semaphore_wait(pltpu.get_barrier_semaphore(), 2 + g.Z)


def remote(src, dst, sems, i, who):
    return pltpu.make_async_remote_copy(src_ref=src, dst_ref=dst, send_sem=sems.at[0, i], recv_sem=sems.at[1, i],
                                        device_id=who, device_id_type=pl.DeviceIdType.MESH)


def halves(cols):
    cut = max(cols // 256, 1) * 128
    return pl.ds(0, cut), pl.ds(cut, cols - cut)


class Gather:
    def __init__(self, g, full, sems):
        self.g, self.full, self.sems = g, full, sems
        cols = full.shape[4]
        self.A, self.B = halves(cols)
        self.whole = cols < 256

    @staticmethod
    def scratch(Z):
        return [pltpu.SemaphoreType.DMA((2, Z - 1 + 5))]

    def lined(self, k):
        own = self.full.at[self.g.block()]
        return remote(own, own, self.sems, k - 1, self.g.at(k=k))

    def col(self, d, part=None):
        ref = self.full.at[self.g.line(d)]
        return ref if part is None else ref.at[:, :, part]

    def far_parts(self):
        return ((-1, 1, self.A), ) if self.whole else ((-1, 1, self.A), (1, -1, self.B))

    def copies(self):
        g = self.g

        def copy(i, ref, who):
            return remote(ref, ref, self.sems, g.Z - 1 + i, who)
        out = {0: copy(0, self.col(0), g.at(1)), 1: copy(1, self.col(0), g.at(-1)), 4: copy(4, self.full.at[:, g.core], g.sibling())}
        for i, (d, to, part) in enumerate(self.far_parts()):
            out[2 + i] = copy(2 + i, self.col(d, part), g.at(to))
        return out

    def arrive(self, i, ref):
        remote(ref, ref, self.sems, i, self.g.sibling()).wait_recv()

    def L(self):
        for k in range(1, self.g.Z):
            self.lined(k).start()

    def N(self):
        g = self.g
        for k in range(1, g.Z):
            self.arrive(k - 1, self.full.at[g.block(k=-k)])
        c = self.copies()
        c[0].start()
        c[1].start()

    def F(self):
        c, n = self.copies(), self.g.Z - 1
        self.arrive(n, self.col(-1))
        c[2].start()
        self.arrive(n + 1, self.col(1))
        if not self.whole:
            c[3].start()

    def T(self):
        n = self.g.Z - 1
        for i, (d, to, part) in enumerate(self.far_parts()):
            self.arrive(n + 2 + i, self.col(2 * d, part))
        self.copies()[4].start()

    def E(self):
        g = self.g
        self.arrive(g.Z - 1 + 4, self.full.at[:, 1 - g.core])
        for k in range(1, g.Z):
            self.lined(k).wait_send()
        for c in self.copies().values():
            c.wait_send()


class Scatter:
    def __init__(self, g, part, write, bufs, sems):
        self.g, self.part, self.write, self.sems = g, part, write, sems
        self.sib, self.ra, self.rb, self.rl, self.rr, self.rz = bufs
        cols = part.shape[4]
        self.A, self.B = halves(cols)
        self.whole = cols < 256

    @staticmethod
    def scratch(Z, rows, cols, dtype):
        a, b = halves(cols)
        shapes = [(4, Z, rows, cols), (Z, rows, a.size), (Z, rows, max(b.size, LANES)), (Z, rows, cols), (Z, rows, cols), (max(Z - 1, 1), rows, cols)]
        return [pltpu.VMEM(s, dtype) for s in shapes] + [pltpu.SemaphoreType.DMA((2, 5 + Z - 1))]

    def cores(self):
        g = self.g
        return remote(self.part.at[:, 1 - g.core], self.sib, self.sems, 0, g.sibling())

    def far(self):
        g = self.g
        src = self.part.at[g.line(2)]
        a = [remote(src.at[:, :, self.A], self.ra, self.sems, 1, g.at(1))]
        return a if self.whole else a + [remote(src.at[:, :, self.B], self.rb, self.sems, 2, g.at(-1))]

    def near(self):
        g = self.g
        return [remote(self.part.at[g.line(1)], self.rl, self.sems, 3, g.at(1)), remote(self.part.at[g.line(-1)], self.rr, self.sems, 4, g.at(-1))]

    def lines(self):
        g = self.g
        return [remote(self.part.at[g.block(k=k)], self.rz.at[k - 1], self.sems, 4 + k, g.at(k=k)) for k in range(1, g.Z)]

    def add(self, d, got=(), part=slice(None)):
        place, core = self.g.line(d)
        s = self.part[place, core, :, :, part].astype(F32) + self.sib[place, :, :, part].astype(F32)
        for t in got:
            s += t[...].astype(F32)
        self.part[place, core, :, :, part] = s.astype(self.part.dtype)

    def B_(self):
        self.cores().start()

    def F(self):
        self.cores().wait_recv()
        self.add(2)
        for c in self.far():
            c.start()

    def N(self):
        for c in self.far():
            c.wait_recv()
        if self.whole:
            self.add(1, [self.ra])
            self.add(-1)
        else:
            self.add(1, [self.ra], self.A)
            self.add(1, (), self.B)
            self.add(-1, [self.rb], self.B)
            self.add(-1, (), self.A)
        for c in self.near():
            c.start()

    def O(self):
        for c in self.near():
            c.wait_recv()
        self.add(0, [self.rl, self.rr])
        for c in self.lines():
            c.start()

    def E(self):
        for c in self.lines():
            c.wait_recv()
        s = self.part[self.g.block()].astype(F32)
        for k in range(1, self.g.Z):
            s += self.rz[k - 1].astype(F32)
        self.write(s)
        for c in [self.cores()] + self.far() + self.near() + self.lines():
            c.wait_send()


def talk(schedule, step, point, points):
    for at, calls in schedule.items():
        if at % points == point:
            @pl.when(step == at // points)
            def _():
                for call in calls:
                    call()


def places(sides_ref, slot, rows):
    a, b, c = sides_ref[slot, 0], sides_ref[slot, 1], sides_ref[slot, 2]
    e1 = a * a
    e2 = e1 + b * b
    e3 = e2 + c * c
    r = lax.broadcasted_iota(jnp.int32, (1, rows), 1)
    in2, in3, out = r >= e1, r >= e2, r >= e3
    seg = in2.astype(jnp.int32) + in3.astype(jnp.int32) + out.astype(jnp.int32)
    start = jnp.where(in3, e2, jnp.where(in2, e1, 0))
    side = jnp.where(in3, c, jnp.where(in2, b, a))
    side = jnp.maximum(side, 1).astype(F32)
    offset = (r - start).astype(F32)
    height = jnp.floor((offset + 0.5) / side)
    across = offset - height * side
    return seg, jnp.where(out, 0.0, height), jnp.where(out, 0.0, across)


def stats(x):
    mean = jnp.mean(x, axis=-1, keepdims=True)
    cen = x - mean
    var = jnp.mean(cen * cen, axis=-1, keepdims=True)
    rstd = lax.rsqrt(var + EPS)
    return cen * rstd, rstd


def ln_back(dn, gain, xhat, rstd):
    e = dn * gain
    m1 = jnp.mean(e, axis=-1, keepdims=True)
    m2 = jnp.mean(e * xhat, axis=-1, keepdims=True)
    return rstd * (e - m1 - xhat * m2)


def flat(w):
    return w.reshape(-1, w.shape[-1])


def unflat(w, like):
    return w.reshape(*like, -1, w.shape[1])


ROWS = ("gain", "shift", "out_bias", "freq", "gain_two", "shift_two", "down_bias", "qkv_bias", "up_bias")


def vectors(small, r, nb, nu):
    n = small.shape[0]
    rows = jnp.concatenate([small[i, 0:8, :r] for i in range(n)], axis=1)
    qkv = jnp.concatenate([small[i, 0:8, :nb * r] for i in range(n)], axis=1)
    up = jnp.concatenate([small[i, 8:16, :nu * r] for i in range(n)], axis=1)
    return rows, qkv, up


def spread(rows, qkv, up, n, store):
    r, rq, ru = rows.shape[1] // n, qkv.shape[1] // n, up.shape[1] // n
    wide = lambda x: jnp.concatenate([x, jnp.zeros((x.shape[0], LANES - x.shape[1]), F32)], axis=1)
    for i in range(n):
        store(i, jnp.concatenate([wide(rows[0:7, i * r:(i + 1) * r]), wide(qkv[:, i * rq:(i + 1) * rq]), wide(up[:, i * ru:(i + 1) * ru]),
                                  jnp.zeros((7, LANES), F32)], axis=0))


def attn_fwd_kernel(plan, *refs):
    sides, tok, *refs = refs
    quad, slot = pl.program_id(0), pl.program_id(1)
    step = quad * pl.num_programs(1) + slot
    schedule = {}
    if plan:
        dp, fsdp, r, nb, nu = plan
        wqkv, wo, up, dnT, small, *refs = refs
        qT, kT, vT, eT, linv, oT, cosT, sinT, rows, urow, wqkv_all, wo_all, chunks, *refs = refs
        n1, trig, w, bcol, fcol, small_all, local, *sems = refs
        g = Grid(dp, fsdp)
        own = g.block()
        mines = []

        def mine(src, dst):
            mines.append(pltpu.make_async_copy(src, dst, local.at[len(mines)]))
        mine(small, small_all.at[own])
        mine(wo, wo_all.at[own])
        for i in range(GROUPS):
            for j in range(3):
                mine(wqkv.at[:, pl.ds((j * GROUPS + i) * GW, GW)], w.at[(i, *own)].at[:, pl.ds(j * GW, GW)])
        for f in range(FIRST):
            for j, src in enumerate((up, dnT)):
                mine(src.at[:, pl.ds(f * CHUNK, CHUNK)], chunks.at[(f, *own)].at[:, pl.ds(j * CHUNK, CHUNK)])
        saves = [pltpu.make_async_copy(w.at[i], wqkv_all.at[i], local.at[len(mines) + i]) for i in range(GROUPS)]
        wholes = [small_all, *(w.at[i] for i in range(GROUPS)), wo_all, *(chunks.at[f] for f in range(FIRST))]
        s, *rest = [Gather(g, a, b) for a, b in zip(wholes, sems)]
        q, o, c = rest[:GROUPS], rest[GROUPS], rest[GROUPS + 1:]

        def ready(a, b):
            for m in mines[a:b]:
                m.wait()

        def begin():
            for m in mines:
                m.start()
            greet(g)

        def then():
            ready(0, 1)
            ready(2, 5)
            met(g)
            s.L()
            q[0].L()
            ready(5, 2 + 3 * GROUPS)
            for call in (s.N, q[0].N, q[1].L, s.F, q[0].F, s.T, q[0].T, q[1].N, q[2].L, s.E, q[0].E, saves[0].start):
                call()
            sm = small_all[...].astype(F32).reshape(-1, 16, LANES)
            vec, qkv, upb = vectors(sm, r, nb, nu)
            rows[...] = vec
            urow[...] = upb
            bcol[...] = qkv.T[:, 7:8]
            fcol[...] = vec.T[:, 3:4]

        chunk = lambda f: functools.partial(ready, 2 + 3 * GROUPS + 2 * f, 4 + 3 * GROUPS + 2 * f)
        schedule = {
            0: [chunk(0), c[0].L],
            1: [chunk(2), c[2].L, q[2].N],
            2: [q[1].F, chunk(1), c[1].L, c[0].N, functools.partial(ready, 1, 2), o.L],
            3: [q[2].F, q[1].T],
            4: [q[1].E, saves[1].start, c[2].N],
            5: [c[1].N],
            6: [c[0].F, o.N, q[2].T],
            7: [q[2].E, saves[2].start],
            8: [c[1].F],
            9: [c[0].T, c[2].F],
            10: [o.F],
            11: [c[1].T, c[2].T, c[0].E, o.T],
        }
        finish = [c[1].E, c[2].E, o.E, *(x.wait for x in saves)]
        weight = lambda: flat(w[quad])
    else:
        w, rows, bcol, fcol, qT, kT, vT, eT, linv, oT, cosT, sinT, n1, trig = refs
        weight = lambda: flat(w[0])
    t = tok.shape[1]

    @pl.when(step == 0)
    def _():
        if plan:
            begin()
        for i in range(tok.shape[0]):
            n1[i] = stats(tok[i].astype(F32))[0]
        if plan:
            then()
        for i in range(tok.shape[0]):
            n1[i] = n1[i] * rows[0:1, :] + rows[1:2, :]

    talk(schedule, step, 0, 2)
    seg, height, across = places(sides, slot, t)

    @pl.when(slot == 0)
    def _():
        lane = lax.broadcasted_iota(jnp.int32, (GW // 2, LANES), 1).astype(F32)
        low = pl.ds(pl.multiple_of(quad * (GW // 2), GW // 2), GW // 2)
        high = pl.ds(pl.multiple_of(fcol.shape[0] // 2 + quad * (GW // 2), GW // 2), GW // 2)
        angle = jnp.where(lane < PLACES, fcol[low] * lane, fcol[high] * (lane - PLACES))
        rest = jnp.concatenate([jnp.cos(angle), jnp.sin(angle)], axis=0)[:, :2 * PLACES]
        parts = []
        for _ in range(3):
            parts.append(rest.astype(BF16))
            rest = rest - parts[-1].astype(F32)
        trig[...] = jnp.concatenate(parts + [jnp.zeros_like(parts[0])], axis=1)

    k256 = lax.broadcasted_iota(jnp.int32, (8 * PLACES, t), 0) % (2 * PLACES)
    pick = lambda v: jnp.where(k256 == v, 1.0, 0.0).astype(BF16)
    by_height = dot(trig[...], pick(height.astype(jnp.int32)), 1, 0)
    by_across = dot(trig[...], pick(across.astype(jnp.int32) + PLACES), 1, 0)
    ch, sh, ca, sa = by_height[:GW // 2], by_height[GW // 2:], by_across[:GW // 2], by_across[GW // 2:]
    cos = ch * ca - sh * sa
    sin = sh * ca + ch * sa
    cosT[0] = cos
    sinT[0] = sin
    j16 = lax.broadcasted_iota(jnp.int32, (16, t), 0)
    hit = j16 == seg
    k_aug = jnp.where(hit, 1.0, 0.0).astype(BF16)
    q_aug = jnp.where(hit | (j16 > 3), 0.0, MASKED).astype(BF16)
    n = n1[slot].astype(BF16)
    x = dot(weight(), n, 0, 1)
    nd = bcol.shape[0] // 3
    bias = jnp.concatenate([bcol[pl.ds(pl.multiple_of(j * nd + quad * GW, GW), GW)] for j in range(3)], axis=0)
    x = x + bias
    xq, xk, xv = x[:GW], x[GW:2 * GW], x[2 * GW:].astype(BF16)
    vT[0] = xv
    qs, ks = [], []
    for h in range(GROUP):
        c_, s_ = cos[h * HALF:(h + 1) * HALF], sin[h * HALF:(h + 1) * HALF]
        lo, mi, hi = h * HD, h * HD + HALF, (h + 1) * HD
        q_ = jnp.concatenate([(xq[lo:mi] * c_ - xq[mi:hi] * s_) * SCALE, (xq[lo:mi] * s_ + xq[mi:hi] * c_) * SCALE], axis=0).astype(BF16)
        k_ = jnp.concatenate([xk[lo:mi] * c_ - xk[mi:hi] * s_, xk[lo:mi] * s_ + xk[mi:hi] * c_], axis=0).astype(BF16)
        qT[0, lo:hi] = q_
        kT[0, lo:hi] = k_
        qs.append(jnp.concatenate([q_, q_aug], axis=0))
        ks.append(jnp.concatenate([k_, k_aug], axis=0))
    sT = dot(ks[0], qs[0], 0, 0)
    for h in range(GROUP):
        if h == GROUP // 2:
            talk(schedule, step, 1, 2)
        now = sT
        if h + 1 < GROUP:
            sT = dot(ks[h + 1], qs[h + 1], 0, 0)
        lo, hi = h * HD, (h + 1) * HD
        m = jnp.max(now, axis=0, keepdims=True)
        e = jnp.exp(now - m)
        inv = 1.0 / jnp.sum(e, axis=0, keepdims=True)
        e = e.astype(BF16)
        eT[h] = e
        linv[0, h:h + 1] = inv
        oT[0, lo:hi] = (dot(xv[lo:hi], e, 1, 0) * inv).astype(BF16)
    linv[0, GROUP:] = jnp.zeros_like(linv[0, GROUP:])
    if plan:
        talk({0: finish}, step - 2 * GROUPS + 1, 0, 1)


def attn_fwd(mesh, sides, tok, args, hand):
    slots, t, d = tok.shape
    fixed = lambda s: pl.BlockSpec(s, lambda i, j: (0,) * len(s))
    tr = pl.BlockSpec((1, GW, t), lambda i, j: (j, i, 0))
    trh = pl.BlockSpec((1, GW // 2, t), lambda i, j: (j, i, 0))
    specs = [tr, tr, tr, pl.BlockSpec((GROUP, t, t), lambda i, j: (j * GROUPS + i, 0, 0)),
             pl.BlockSpec((1, 8, t), lambda i, j: (j * GROUPS + i, 0, 0)), tr, trh, trh]
    shapes = [SD((slots, d, t), BF16)] * 3 + [SD((slots * HEADS, t, t), BF16), SD((slots * GROUPS, 8, t), F32), SD((slots, d, t), BF16)]
    shapes += [SD((slots, d // 2, t), F32)] * 2
    scratch = [pltpu.VMEM((slots, t, d), F32), pltpu.VMEM((GW, 8 * PLACES), BF16)]
    plan, params = None, {}
    if hand:
        dp, fsdp = mesh.shape["dp"], mesh.shape["fsdp"]
        wqkv, wo, up, dnT, small = args
        r = wqkv.shape[0]
        nb, nu = wqkv.shape[1] // d, up.shape[1] // d
        plan = dp, fsdp, r, nb, nu
        in_specs = [ANY] * 5
        specs += [fixed((8, d)), fixed((8, up.shape[1])), ANY, ANY, ANY]
        n = dp // 2, 2, fsdp
        shapes += [SD((8, d), F32), SD((8, up.shape[1]), F32), SD((GROUPS, *n, r, 3 * GW), BF16), SD((*n, r, d), BF16), SD((FIRST, *n, r, 2 * CHUNK), BF16)]
        scratch += [pltpu.VMEM((GROUPS, *n, r, 3 * GW), BF16), pltpu.VMEM((nb * d, 1), F32), pltpu.VMEM((d, 1), F32), pltpu.VMEM((*n, 16, LANES), BF16),
                    pltpu.SemaphoreType.DMA((2 + 4 * GROUPS + 2 * FIRST,))]
        scratch += Gather.scratch(fsdp) * (2 + GROUPS + FIRST)
        params = dict(collective_id=0, has_side_effects=True)
    else:
        w, rows, bcol, fcol = args
        in_specs = [pl.BlockSpec((1, d, 3 * GW), lambda i, j: (i, 0, 0)), fixed(rows.shape), fixed(bcol.shape), fixed(fcol.shape)]
    return pl.pallas_call(
        functools.partial(attn_fwd_kernel, plan),
        grid=(GROUPS, slots),
        in_specs=[pl.BlockSpec(memory_space=pltpu.SMEM), fixed(tok.shape), *in_specs],
        out_specs=specs, out_shape=shapes, scratch_shapes=scratch,
        compiler_params=pltpu.CompilerParams(vmem_limit_bytes=60 * 2**20, **params),
        name="attn_fwd",
    )(sides, tok, *args)


def mlp_kernel(plan, *refs):
    tok, oT, wo, g_, rows, ub, *refs = refs
    f, last = pl.program_id(0), pl.num_programs(0) - 1
    schedule = {}
    if plan:
        dp, fsdp, count = plan
        chunks, up, dnT, out, mgrad, small, dub, dwo, late, early, *refs = refs
        w, local, n2, act, hg, oacc, dacc, *refs = refs
        g = Grid(dp, fsdp)
        mines = [pltpu.make_async_copy(src.at[:, pl.ds((FIRST + i) * CHUNK, CHUNK)], w.at[(FIRST + i, *g.block())].at[:, pl.ds(j * CHUNK, CHUNK)],
                                       local.at[2 * i + j])
                 for i in range(count - FIRST) for j, src in enumerate((up, dnT))]
        loads = [pltpu.make_async_copy(chunks.at[i], w.at[i], local.at[len(mines) + i]) for i in range(FIRST)]
        outs = [pltpu.make_async_copy(w.at[i], late.at[i - EARLY], local.at[len(mines) + i]) for i in range(EARLY, count)]
        c = {FIRST + i: Gather(g, w.at[FIRST + i], refs[i]) for i in range(count - FIRST)}
        refs = refs[count - FIRST:]

        def keep(i):
            def write(s):
                early[i] = s
            return write
        rs = [Scatter(g, w.at[i], keep(i), refs[7 * i:7 * i + 6], refs[7 * i + 6]) for i in range(EARLY)]

        def begin():
            for m in loads + mines:
                m.start()
            greet(g)

        def then():
            for m in mines:
                m.wait()
            met(g)
            c[3].L()
            loads[0].wait()
        schedule = {
            0: [c[4].L],
            4: [loads[1].wait, c[3].N, c[5].L],
            5: [rs[0].B_, c[4].N],
            7: [rs[0].F],
            8: [loads[2].wait, c[3].F],
            9: [rs[1].B_, c[4].F, c[5].N],
            10: [c[3].T, rs[1].F, rs[0].N],
            11: [c[4].T],
            12: [c[3].E, rs[2].B_],
            13: [c[4].E, rs[2].F],
            14: [c[5].F],
            16: [rs[1].N, rs[0].O, outs[0].start],
            17: [c[5].T, rs[2].N],
            19: [c[5].E],
            20: [rs[1].O, outs[1].start],
            21: [rs[2].O],
            22: [rs[0].E],
        }
        finish = [outs[2].start], [rs[2].E, rs[1].E, *(x.wait for x in outs)]
        weight = lambda: w[f]
    else:
        w, out, mgrad, small, dub, dwo, dw, n2, act, hg, oacc, dacc = refs
        weight = lambda: w[0]
    mid = mgrad

    @pl.when(f == 0)
    def _():
        if plan:
            begin()
        slots = oT.shape[0]
        branch = jnp.concatenate([dot(oT[i], flat(wo[...]), 0, 0) for i in range(slots)], axis=0)
        x = tok[...].astype(F32) + branch + rows[2:3, :]
        mid[...] = x
        xhat, _ = stats(x)
        n2[...] = (xhat * rows[4:5, :] + rows[5:6, :]).astype(BF16)
        oacc[...] = x + rows[6:7, :]
        if plan:
            then()

    talk(schedule, f, 0, 4)
    v = dot(n2[...], flat(weight()[..., :CHUNK]), 1, 0) + ub[0:1, :]
    ga = dot(g_[...], flat(weight()[..., CHUNK:]), 1, 0)
    v2 = v * v
    t = jnp.tanh(v * (GELU_A + GELU_B * v2))
    p = 0.5 * t + 0.5
    act[...] = (v * p).astype(BF16)
    slope = p + (0.5 * v) * (1.0 - t * t) * (GELU_A + (3.0 * GELU_B) * v2)
    low = (slope * ga).astype(BF16)
    hg[...] = low
    dub[...] = jnp.sum(low.astype(F32), axis=0, keepdims=True)
    talk(schedule, f, 1, 4)
    oacc[...] += dot(act[...], flat(weight()[..., CHUNK:]), 1, 1)
    dn = dot(hg[...], flat(weight()[..., :CHUNK]), 1, 1)

    @pl.when(f == 0)
    def _():
        dacc[...] = dn

    @pl.when(f > 0)
    def _():
        dacc[...] += dn

    talk(schedule, f, 2, 4)
    for point, cols, a, b in ((3, slice(0, CHUNK), n2, hg), (None, slice(CHUNK, None), g_, act)):
        grad = dot(a[...], b[...], 0, 0)
        if plan:
            w[f, :, :, :, :, cols] = unflat(grad, w.shape[1:4]).astype(BF16)
        else:
            dw[0, :, cols] = grad.astype(BF16)
        if point:
            talk(schedule, f, point, 4)

    @pl.when(f == last)
    def _():
        if plan:
            for call in finish[0]:
                call()
        out[...] = oacc[...].astype(BF16)
        xhat, rstd = stats(mid[...])
        dn = dacc[...]
        gf = g_[...].astype(F32)
        mg = gf + ln_back(dn, rows[4:5, :], xhat, rstd)
        mgrad[...] = mg
        low = mg.astype(BF16)
        small[4:5, :] = jnp.sum(dn * xhat, axis=0, keepdims=True)
        small[5:6, :] = jnp.sum(dn, axis=0, keepdims=True)
        small[6:7, :] = jnp.sum(gf, axis=0, keepdims=True)
        small[2:3, :] = jnp.sum(low.astype(F32), axis=0, keepdims=True)
        small[0:2, :] = jnp.zeros_like(small[0:2, :])
        small[3:4, :] = jnp.zeros_like(small[3:4, :])
        small[7:8, :] = jnp.zeros_like(small[7:8, :])
        slots, t = oT.shape[0], oT.shape[2]
        go = dot(oT[0], mg[:t].astype(BF16), 1, 0)
        for i in range(1, slots):
            go += dot(oT[i], mg[i * t:(i + 1) * t].astype(BF16), 1, 0)
        dwo[...] = (unflat(go, dwo.shape[:3]) if plan else go).astype(BF16)
        if plan:
            for call in finish[1]:
                call()


def mlp(mesh, tok, oT, wo, g, rows, urow, args, hand):
    t, d = tok.shape
    ff = urow.shape[1]
    count = ff // CHUNK
    fixed = lambda s: pl.BlockSpec(s, lambda f: (0,) * len(s), pipeline_mode=pl.Buffered(1))
    col = lambda h: pl.BlockSpec((h, CHUNK), lambda f: (0, f))
    specs = [fixed((t, d)), fixed((t, d)), fixed((8, d)), col(1), fixed(wo.shape)]
    shapes = [SD((t, d), BF16), SD((t, d), F32), SD((8, d), F32), SD((1, ff), F32), SD(wo.shape, BF16)]
    scratch = [pltpu.VMEM((t, d), BF16), pltpu.VMEM((t, CHUNK), BF16), pltpu.VMEM((t, CHUNK), BF16), pltpu.VMEM((t, d), F32), pltpu.VMEM((t, d), F32)]
    plan, params = None, {}
    if hand:
        dp, fsdp = mesh.shape["dp"], mesh.shape["fsdp"]
        chunks, up, dnT = args
        *n, r, w2 = chunks.shape[1:]
        plan = dp, fsdp, count
        in_specs = [ANY] * 3
        specs += [ANY, fixed((EARLY, r, w2))]
        shapes += [SD((count - EARLY, *n, r, w2), BF16), SD((EARLY, r, w2), F32)]
        scratch = [pltpu.VMEM((count, *n, r, w2), BF16), pltpu.SemaphoreType.DMA((2 * (count - FIRST) + count,)), *scratch]
        scratch += Gather.scratch(fsdp) * (count - FIRST) + Scatter.scratch(fsdp, r, w2, BF16) * EARLY
        params = dict(collective_id=1, has_side_effects=True)
    else:
        wide = pl.BlockSpec((1, d, 2 * CHUNK), lambda f: (f, 0, 0))
        in_specs = [wide]
        specs += [wide]
        shapes += [SD((count, d, 2 * CHUNK), BF16)]
    return pl.pallas_call(
        functools.partial(mlp_kernel, plan),
        grid=(count,),
        in_specs=[fixed((t, d)), fixed(oT.shape), fixed(wo.shape), fixed((t, d)), fixed((8, d)), col(8), *in_specs],
        out_specs=specs, out_shape=shapes, scratch_shapes=scratch,
        compiler_params=pltpu.CompilerParams(vmem_limit_bytes=62 * 2**20, **params),
        name="mlp",
    )(tok, oT, wo, g, rows, urow, *args)


def attn_bwd_kernel(plan, *refs):
    sides, tok, mgrad, w, wo, rows, qT, kT, vT, eT, linv, oT, cosT, sinT, *refs = refs
    quad, slot = pl.program_id(0), pl.program_id(1)
    lastq, lasts = pl.num_programs(0) - 1, pl.num_programs(1) - 1
    step = quad * pl.num_programs(1) + slot
    schedule = {}
    tail = [[]] * 3
    if plan:
        dp, fsdp = plan
        small2, dub, dwo, late, tgrad, gqkv, go, gs, gl, *refs = refs
        n1, dacc, mg, vec, qb, px, po, pq, ps, local, *refs = refs
        g = Grid(dp, fsdp)
        count = late.shape[0]
        loads = [pltpu.make_async_copy(late.at[i], px.at[i], local.at[i]) for i in range(count)] + [pltpu.make_async_copy(dwo, po, local.at[count])]
        units = []

        def unit(part, write):
            nonlocal refs
            units.append(Scatter(g, part, write, refs[:6], refs[6]))
            refs = refs[7:]
            return units[-1]

        def into(ref, i=None):
            def write(s):
                if i is None:
                    ref[...] = s
                else:
                    ref[i] = s
            return write
        x = [unit(px.at[i], into(gl, i)) for i in range(count)]
        o = unit(po, into(go))

        def quads(i):
            def write(s):
                for j in range(3):
                    gqkv[:, (j * GROUPS + i) * GW:(j * GROUPS + i + 1) * GW] = s[:, j * GW:(j + 1) * GW]
            return write
        q = [unit(pq.at[i], quads(i)) for i in range(GROUPS)]
        sm = unit(ps, into(gs))

        def begin():
            for m in loads:
                m.start()
            greet(g)

        def then():
            met(g)
            loads[-1].wait()
            o.B_()

        schedule = {
            1: [loads[0].wait, x[0].B_, loads[1].wait, x[1].B_],
            3: [o.F, x[0].F, loads[2].wait, x[2].B_],
            4: [x[1].F],
            5: [x[2].F, o.N],
            6: [q[0].B_, x[0].N],
            7: [x[2].N, q[0].F],
            9: [x[0].O, x[1].N],
            12: [q[1].B_, o.O],
            13: [q[1].F, x[2].O, x[1].O, q[0].N],
            14: [q[1].N],
            15: [q[0].O],
            16: [x[0].E, q[1].O, x[2].E],
            17: [o.E],
        }
        tail = [[q[2].B_], [sm.B_, q[2].F, sm.F, q[0].E, x[1].E, q[2].N, sm.N, q[1].E, q[2].O, sm.O, q[2].E, sm.E]]
        weight = lambda: flat(w[0])
    else:
        tgrad, dwqkv, vec, qb, n1, dacc, mg = refs
        weight = lambda: flat(w[0])
    t = tok.shape[1]

    @pl.when(step == 0)
    def _():
        if plan:
            begin()
        for i in range(tok.shape[0]):
            xhat, _ = stats(tok[i].astype(F32))
            n1[i] = (xhat * rows[0:1, :] + rows[1:2, :]).astype(BF16)
        vec[...] = small2[...] if plan else jnp.zeros_like(vec)
        qb[...] = jnp.zeros_like(qb)
        if plan:
            then()

    talk(schedule, step, 0, 3)
    _, height, across = places(sides, slot, t)
    ml = mgrad[slot].astype(BF16)
    wo_q = pl.ds(pl.multiple_of(quad * GW, GW), GW)
    dO = dot(wo[wo_q], ml, 1, 1)
    dqs, dks, dvs, angs = [], [], [], []
    for h in range(GROUP):
        if h == GROUP // 2:
            talk(schedule, step, 1, 3)
        lo, mi, hi = h * HD, h * HD + HALF, (h + 1) * HD
        c_, s_ = cosT[0, h * HALF:(h + 1) * HALF], sinT[0, h * HALF:(h + 1) * HALF]
        dof = dO[lo:hi] * linv[0, h:h + 1]
        do = dof.astype(BF16)
        dd = jnp.sum(dof * oT[0, lo:hi].astype(F32), axis=0, keepdims=True)
        dp_ = dot(vT[0, lo:hi], do, 0, 0)
        e = eT[h]
        ds = (e.astype(F32) * (dp_ - dd)).astype(BF16)
        dvs.append(dot(do, e, 1, 1))
        dk = dot(qT[0, lo:hi], ds, 1, 1)
        dq = dot(kT[0, lo:hi], ds, 1, 0)
        k = kT[0, lo:hi].astype(F32)
        q_ = qT[0, lo:hi].astype(F32)
        angs.append(dq[HALF:] * q_[:HALF] - dq[:HALF] * q_[HALF:] + dk[HALF:] * k[:HALF] - dk[:HALF] * k[HALF:])
        dq = dq * SCALE
        dqs += [dq[:HALF] * c_ + dq[HALF:] * s_, dq[HALF:] * c_ - dq[:HALF] * s_]
        dks += [dk[:HALF] * c_ + dk[HALF:] * s_, dk[HALF:] * c_ - dk[:HALF] * s_]
    m = jnp.concatenate(dqs + dks + dvs, axis=0).astype(BF16)
    mg[slot] = m
    ang = jnp.concatenate(angs, axis=0)
    j8 = lax.broadcasted_iota(jnp.int32, (8, t), 0)
    where = jnp.where(j8 == 0, height, jnp.where(j8 == 1, across, 0.0)).astype(BF16)
    big = ang.astype(BF16)
    fr = dot(where, big, 1, 1) + dot(where, (ang - big.astype(F32)).astype(BF16), 1, 1)
    d = vec.shape[1]
    for a in range(2):
        at = pl.ds(pl.multiple_of(a * (d // 2) + quad * (GW // 2), GW // 2), GW // 2)
        vec[3:4, at] += fr[a:a + 1]
    bias = dot(jnp.ones((8, t), BF16), m, 1, 1)[0:1]
    for j in range(3):
        at = pl.ds(pl.multiple_of(j * d + quad * GW, GW), GW)
        qb[0:1, at] += bias[:, j * GW:(j + 1) * GW]
    talk(schedule, step, 2, 3)

    @pl.when(slot == lasts)
    def _():
        gw = dot(n1[0], mg[0], 0, 1)
        for i in range(1, n1.shape[0]):
            gw += dot(n1[i], mg[i], 0, 1)
        if plan:
            pq[quad] = unflat(gw, pq.shape[1:4]).astype(BF16)
        else:
            dwqkv[0] = gw.astype(BF16)

    if plan:
        @pl.when((quad == lastq) & (slot == lasts))
        def _():
            for call in tail[0]:
                call()

    dn = dot(m, weight(), 0, 1)

    @pl.when(quad == 0)
    def _():
        dacc[slot] = dn

    @pl.when(quad > 0)
    def _():
        dacc[slot] += dn

    @pl.when(quad == lastq)
    def _():
        xhat, rstd = stats(tok[slot].astype(F32))
        dn = dacc[slot]
        tgrad[slot] = (mgrad[slot] + ln_back(dn, rows[0:1, :], xhat, rstd)).astype(BF16)
        vec[0:1, :] += jnp.sum(dn * xhat, axis=0, keepdims=True)
        vec[1:2, :] += jnp.sum(dn, axis=0, keepdims=True)

    if plan:
        @pl.when((quad == lastq) & (slot == lasts))
        def _():
            cs, zs = ps.shape[1:3]

            def store(i, x):
                ps[i // (cs * zs), i // zs % cs, i % zs] = x
            spread(vec[...], qb[0:1, :], dub[...], dp * fsdp, store)
            for call in tail[1]:
                call()


def attn_bwd(mesh, sides, tok, mgrad, w, wo, rows, saved, args, hand):
    slots, t, d = tok.shape
    fixed = lambda s: pl.BlockSpec(s, lambda i, j: (0,) * len(s), pipeline_mode=pl.Buffered(1))
    tr = pl.BlockSpec((1, GW, t), lambda i, j: (j, i, 0))
    trh = pl.BlockSpec((1, GW // 2, t), lambda i, j: (j, i, 0))
    block = lambda s: pl.BlockSpec((1, *s[1:]), lambda i, j: (i,) + (0,) * (len(s) - 1))
    specs = [fixed(tok.shape)]
    shapes = [SD(tok.shape, BF16)]
    scratch = [pltpu.VMEM((slots, t, d), BF16), pltpu.VMEM((slots, t, d), F32), pltpu.VMEM((slots, 3 * GW, t), BF16)]
    vec, qb = (8, d), (8, 3 * d)
    plan, params = None, {}
    if hand:
        dp, fsdp = mesh.shape["dp"], mesh.shape["fsdp"]
        small2, dub, dwo, late = args
        *n, r, _ = dwo.shape
        plan = dp, fsdp
        in_specs = [fixed(small2.shape), fixed(dub.shape), ANY, ANY]
        outs = [(r, 3 * d), (r, d), (16, LANES), (late.shape[0], *late.shape[4:])]
        specs += [fixed(s) for s in outs]
        shapes += [SD(s, F32) for s in outs]
        parts = [*[late.shape[1:]] * late.shape[0], dwo.shape, *[(*n, r, 3 * GW)] * GROUPS]
        scratch += [pltpu.VMEM(vec, F32), pltpu.VMEM(qb, F32), pltpu.VMEM(late.shape, BF16), pltpu.VMEM(dwo.shape, BF16),
                    pltpu.VMEM((GROUPS, *n, r, 3 * GW), BF16), pltpu.VMEM((*n, 16, LANES), F32), pltpu.SemaphoreType.DMA((late.shape[0] + 1,))]
        scratch += [y for s in parts for y in Scatter.scratch(fsdp, s[3], s[4], BF16)] + Scatter.scratch(fsdp, 16, LANES, F32)
        params = dict(collective_id=2, has_side_effects=True)
    else:
        in_specs = []
        specs += [block((GROUPS, d, 3 * GW)), fixed(vec), fixed(qb)]
        shapes += [SD((GROUPS, d, 3 * GW), BF16), SD(vec, F32), SD(qb, F32)]
    return pl.pallas_call(
        functools.partial(attn_bwd_kernel, plan),
        grid=(GROUPS, slots),
        in_specs=[pl.BlockSpec(memory_space=pltpu.SMEM), fixed(tok.shape), fixed(tok.shape), block(w.shape), fixed((d, d)), fixed((8, d)),
                  tr, tr, tr, pl.BlockSpec((GROUP, t, t), lambda i, j: (j * GROUPS + i, 0, 0)), pl.BlockSpec((1, 8, t), lambda i, j: (j * GROUPS + i, 0, 0)),
                  tr, trh, trh, *in_specs],
        out_specs=specs, out_shape=shapes, scratch_shapes=scratch,
        compiler_params=pltpu.CompilerParams(vmem_limit_bytes=62 * 2**20, **params),
        name="attn_bwd",
    )(sides, tok, mgrad, w, wo, rows, *saved, *args)


def lay_out_kernel(r, widths, gqkv, go, gs, early, late, an_o, qkv_o, bq_o, o_o, bo_o, f_o, mn_o, up_o, bu_o, dT_o, bd_o):
    qkv_o[...] = gqkv[...]
    o_o[...] = go[...]
    for f, ref in enumerate([early.at[i] for i in range(early.shape[0])] + [late.at[i] for i in range(late.shape[0])]):
        up_o[:, f * CHUNK:(f + 1) * CHUNK] = ref[:, :CHUNK]
        dT_o[:, f * CHUNK:(f + 1) * CHUNK] = ref[:, CHUNK:]
    nb, nu = widths
    an_o[...] = gs[0:2, :r]
    bo_o[...] = gs[2:3, :r]
    f_o[...] = gs[3:4, :r]
    mn_o[...] = gs[4:6, :r]
    bd_o[...] = gs[6:7, :r]
    bq_o[...] = gs[7:8, :nb]
    bu_o[...] = gs[8:9, :nu]


def lay_out(gqkv, go, gs, early, late, nb, nu):
    r, d = go.shape
    ff = (early.shape[0] + late.shape[0]) * CHUNK
    one = lambda w: SD((1, w), F32)
    vm = pl.BlockSpec(memory_space=pltpu.VMEM)
    shapes = [SD((2, r), F32), SD(gqkv.shape, F32), one(nb), SD(go.shape, F32), one(r), one(r), SD((2, r), F32),
              SD((r, ff), F32), one(nu), SD((r, ff), F32), one(r)]
    res = pl.pallas_call(
        functools.partial(lay_out_kernel, r, (nb, nu)),
        in_specs=[vm] * 5, out_specs=[vm] * 11, out_shape=shapes, name="lay_out",
    )(gqkv, go, gs, early, late)
    res = list(res)
    res[9] = res[9].T
    return tuple(x.reshape(-1) if x.shape[0] == 1 else x for x in res)


def on_device(mesh, tok, sides, g, attn_norm, wqkv, bqkv, wo, bo, freq, mlp_norm, up, ub, down, db):
    n = mesh.shape["dp"] * mesh.shape["fsdp"]
    slots = sides.shape[0]
    d = tok.shape[1]
    t = tok.shape[0] // slots
    r = wqkv.shape[0]
    ff = up.shape[1]
    nb, nu = bqkv.shape[0] // r, ub.shape[0] // r
    count = ff // CHUNK
    hand = mesh.shape["dp"] == 8 and r % 8 == 0 and count == 6
    dnT = down.T
    small, at = jnp.zeros((16, LANES), BF16), 0
    for x in (attn_norm, bo, freq, mlp_norm, db, bqkv, ub):
        x = x.reshape(-1, x.shape[-1])
        small += jnp.pad(x, ((at, 16 - at - x.shape[0]), (0, LANES - x.shape[1])))
        at += x.shape[0]
    t3 = tok.reshape(slots, t, d)
    if hand:
        *saved, rows, urow, wqkv, wo, chunks = attn_fwd(mesh, sides, t3, (wqkv, wo, up, dnT, small), True)
        out, mgrad, small2, dub, dwo, late, early = mlp(mesh, tok, saved[5], wo, g, rows, urow, (chunks, up, dnT), True)
        tg, gqkv, go, gs, gl = attn_bwd(mesh, sides, t3, mgrad.reshape(t3.shape), wqkv, wo.reshape(d, d), rows, saved, (small2, dub, dwo, late), True)
        return (out, tg.reshape(-1, d)) + lay_out(gqkv, go, gs, early, gl, nb * r, nu * r)
    else:
        whole = lambda x: lax.all_gather(x, BOTH, axis=0, tiled=True)
        wqkv, wo, up, dnT = (whole(x) for x in (wqkv, wo, up, dnT))
        small = lax.all_gather(small, BOTH, axis=0).astype(F32)
        wide = lambda i, k: small[:, i, :k * r].reshape(1, k * d)
        rows = small[:, :8, :r].transpose(1, 0, 2).reshape(8, d)
        urow = jnp.broadcast_to(wide(8, nu), (8, nu * d))
        w = wqkv.reshape(d, 3, GROUPS, GW).transpose(2, 0, 1, 3).reshape(GROUPS, d, 3 * GW)
        saved = attn_fwd(mesh, sides, t3, (w, rows, wide(7, nb).T, rows[3:4].T), False)
        chunks = jnp.stack([up.reshape(d, count, CHUNK), dnT.reshape(d, count, CHUNK)], axis=2).transpose(1, 0, 2, 3).reshape(count, d, 2 * CHUNK)
        out, mgrad, small2, dub, dwo, dw = mlp(mesh, tok, saved[5], wo, g, rows, urow, (chunks,), False)
        tg, dwqkv, vec, qb = attn_bwd(mesh, sides, t3, mgrad.reshape(t3.shape), w, wo, rows, saved, (), False)
        total = lambda x, ax: lax.psum_scatter(x.astype(F32), BOTH, scatter_dimension=ax, tiled=True)
        gqkv = total(dwqkv.reshape(GROUPS, d, 3, GW).transpose(1, 2, 0, 3).reshape(d, 3 * d), 0)
        go = total(dwo, 0)
        both = total(dw, 1)
        cut = lambda x: jnp.pad(x.reshape(x.shape[0], n, -1).transpose(1, 0, 2), ((0, 0), (0, 0), (0, LANES - x.shape[1] // n)))
        gs = total(jnp.concatenate([cut((vec + small2)[:7]), cut(qb[:1]), cut(dub), jnp.zeros((n, 7, LANES), F32)], axis=1), 0)[0]
    gup = both[:, :, :CHUNK].transpose(1, 0, 2).reshape(r, ff)
    gdT = both[:, :, CHUNK:].transpose(1, 0, 2).reshape(r, ff)
    return (out, tg.reshape(-1, d), gs[0:2, :r], gqkv, gs[7, :nb * r], go, gs[2, :r], gs[3, :r], gs[4:6, :r], gup, gs[8, :nu * r], gdT.T, gs[6, :r])


def solution(mesh):
    row, col, one = P(BOTH, None), P(None, BOTH), P(BOTH)
    return jax.shard_map(
        functools.partial(on_device, mesh), mesh=mesh,
        in_specs=(row, row, row, col, row, one, row, one, one, col, row, one, col, one),
        out_specs=(row, row, col, row, one, row, one, one, col, row, one, col, one),
        check_vma=False,
    )
```

time: 941 us -> 215 us (0.23)
  waiting for transfers between devices: 329 us -> 0 us
  matrix products: 235 us -> 0 us
  blocking collectives: 212 us -> 0 us
  Pallas kernels: 0 us -> 210 us
  other arithmetic: 94.4 us -> 1.36 us
  local copies, waits for them, and re-layouts: 47.5 us -> 3.4 us
  between operations: 16.2 us -> 0.68 us
    reduce_scatter x4 -> x0, waiting for transfers between devices: 326 us -> none  [the longest x1 142 us: on_device(): lax.psum_scatter(mlp_total[1], ('dp', 'fsdp'), scatter_dimension=0, tiled...]
    dot_general x36 -> x0, matrix products: 235 us -> none  [the longest x8 55 us: left_product(): lax.dot_general(first_arg, second_arg, (((0,), (0,)), ((), ())), preferre...]
    pallas_call x0 -> x4, Pallas kernels: none -> 210 us  [the longest x1 75.2 us: attn_bwd(): pl.pallas_call(functools.partial(attn_bwd_kernel, plan), grid=(GROUPS, sl...]
    all_gather x2 -> x0, blocking collectives: 129 us -> none  [the longest x1 65.4 us: on_device(): lax.all_gather(attn_norm, ('dp', 'fsdp'), axis=1, tiled=True)]
    unnamed x2 -> x0, blocking collectives: 83.6 us -> none
    reduce_sum x16 -> x0, other arithmetic: 35.5 us -> none  [the longest x2 17.7 us: forward_slot(): row_total = jnp.sum(weights, axis=-1, keepdims=True)]
    convert_element_type x11 -> x0, other arithmetic: 28.8 us -> none  [the longest x2 26.4 us: backward_slot(): (full_probs * (probability_grad - row_inner)).astype(jnp.bfloat16)]
    slice x13 -> x0, local copies, waits for them, and re-layouts: 24.5 us -> none  [the longest x4 13.1 us: forward_slot(): mixed[:, :model_width]]
  transfers between devices with their start and end apart: 8 -> 0, of which waited for: 3 -> 0; matrix products, arithmetic and copies ran while one was open for 28% -> 0% of each run, Pallas kernels for 0% -> 0%
where the time goes in v1:
time: 215 us
  Pallas kernels  210 us (98%)
  local copies, waits for them, and re-layouts  3.4 us (2%)
    pallas_call x1, Pallas kernels, attn_bwd(): pl.pallas_call(functools.partial(attn_bwd_kernel, plan), grid=(GROUPS, sl...  75.2 us
    pallas_call x1, Pallas kernels, mlp(): pl.pallas_call(functools.partial(mlp_kernel, plan), grid=(count,), in_spe...  67.4 us
    pallas_call x1, Pallas kernels, attn_fwd(): pl.pallas_call(functools.partial(attn_fwd_kernel, plan), grid=(GROUPS, sl...  64.8 us

profile of v1, /device:TPU:0, one launch (start us, length us, event | category | flops | bytes accessed | tf_op | source)
XLA Modules:
  0.0 215.0 jit_solution(8985520521301581824)
XLA Ops:
  0.6 1.4 pad_add_fusion.refs_6_
  2.0 64.8 %attn_fwd.1 = (bf16[2,768,600]{2,1,0:T(8,128)(2,1)}, bf16[2,768,600]{2,1,0:T(8,128)(2,1)}, bf16[2,768,600]{2,1,0:T(8,128)(2,1)}, bf16[24,600,600]{2,1,0:T(8,128)...) custom-call(s32[2,3]{1,0:T(2,128)} %refs_0_.5, ...), custom_call_target="tpu_custom_call" | custom-call | tf_op jit(solution)/shard_map/attn_fwd/pallas_call | solution.py:483
  66.8 67.4 %mlp.1 = (bf16[1200,768]{1,0:T(8,128)(2,1)}, f32[1200,768]{1,0:T(8,128)}, f32[8,768]{1,0:T(8,128)}, f32[1,3072]{1,0:T(1,128)}, bf16[4,2,4,24,768]{4,3,2,1,0:T(8,...) custom-call(bf16[1200,768]{1,0:T(8,128)(2,1)} %refs_0_.4, ...), custom_call_target="tpu_custom_call" | custom-call | tf_op jit(solution)/shard_map/mlp/pallas_call | solution.py:655
  134.2 0.0 copy-start
  134.2 75.2 %attn_bwd.1 = (bf16[2,600,768]{2,1,0:T(8,128)(2,1)}, f32[24,2304]{1,0:T(8,128)}, f32[24,768]{1,0:T(8,128)}, f32[16,128]{1,0:T(8,128)}, f32[3,24,1024]{2,1,0:T(8,128)}) custom-call(s32[2,3]{1,0:T(2,128)} %refs_0_.5, bf16[2,600,768]{2,1,0:T(8,128)(2,1)} %bitcast.17, f32[2,600,768]{2,1,0:T(8,128)} %bitcast.19, ...), custom_call_target="tpu_custom_call" | custom-call | tf_op jit(solution)/shard_map/attn_bwd/pallas_call | solution.py:867
  209.4 2.2 %lay_out.1 = (f32[2,24]{1,0:T(2,128)}, f32[24,2304]{1,0:T(8,128)}, f32[1,72]{1,0:T(1,128)}, f32[24,768]{1,0:T(8,128)}, f32[1,24]{1,0:T(1,128)}, /*index=5*/f32[1...) custom-call(f32[24,2304]{1,0:T(8,128)} %get-tuple-element.69.gqkv, ...), custom_call_target="tpu_custom_call" | custom-call | tf_op jit(solution)/shard_map/lay_out/pallas_call | solution.py:902
  211.6 0.0 copy-start.1
  211.6 0.0 copy-done
  211.6 1.2 copy.29
  212.8 0.9 copy-done.1
  213.8 1.2 copy.30
Async XLA Ops:
  134.2 77.4 %copy-start = (bf16[1200,768]{1,0:T(8,128)(2,1)S(1)}, bf16[1200,768]{1,0:T(8,128)(2,1)}, u32[]{:S(2)}) copy-start(bf16[1200,768]{1,0:T(8,128)(2,1)} %get-tuple-element.98) | copy-start | bytes 5529604
  211.6 2.2 %copy-start.1 = (bf16[2,600,768]{2,1,0:T(8,128)(2,1)S(1)}, bf16[2,600,768]{2,1,0:T(8,128)(2,1)}, u32[]{:S(2)}) copy-start(bf16[2,600,768]{2,1,0:T(8,128)(2,1)} %get-tuple-element.68) | copy-start | bytes 5529604

commit v2 on v1

--- a/solution.py
+++ b/solution.py
@@ -14,7 +14,8 @@
 GW = GROUP * HD
 CHUNK = 512
 FIRST = 3
-EARLY = 3
+EARLY = 4
+ENDS = ((0,), (1, 2))
 PLACES = 32
 EPS = 1e-06
 SCALE = 0.125
@@ -37,22 +38,23 @@
     def __init__(self, dp, fsdp):
         self.P, self.Z = dp // 2, fsdp
         i = lax.axis_index("dp")
-        self.core, self.z = i % 2, lax.axis_index("fsdp")
-        self.ring = self.turn(i // 2)
+        self.core, z = i % 2, lax.axis_index("fsdp")
+        ring = self.turn(i // 2)
+        self.places = {d: self.turn((ring + d + self.P) % self.P) for d in (-1, 0, 1, 2)}
+        self.zs = {k: (z + k + fsdp) % fsdp for k in range(1 - fsdp, fsdp)}
 
     def turn(self, p):
         return p + (p // 2) * (5 - 2 * p)
 
     def place(self, d):
-        return self.turn((self.ring + d + self.P) % self.P)
+        return self.places[2 if d == -2 else d]
 
     def at(self, d=0, core=None, k=0):
         core = self.core if core is None else core
-        return (self.place(d) * 2 + core, (self.z + k + self.Z) % self.Z)
+        return (self.place(d) * 2 + core, self.zs[k])
 
     def block(self, d=0, k=0):
-        a, b = self.at(d, None, k)
-        return self.place(d), self.core, b
+        return self.place(d), self.core, self.zs[k]
 
     def line(self, d=0):
         return self.place(d), self.core
@@ -61,14 +63,24 @@
         return self.at(core=1 - self.core)
 
 
-def greet(g):
+def partners(g, wide):
+    if wide:
+        return [g.sibling()] + [g.at(d, k=k) for d, k in others(g)]
+    return [g.at(1), g.at(-1), g.sibling()] + [g.at(k=k) for k in range(1, g.Z)]
+
+
+def others(g):
+    return [(d, k) for d in (0, 1, -1, 2) for k in range(g.Z) if (d, k) != (0, 0)]
+
+
+def greet(g, wide=False):
     barrier = pltpu.get_barrier_semaphore()
-    for w in [g.at(1), g.at(-1), g.sibling()] + [g.at(k=k) for k in range(1, g.Z)]:
+    for w in partners(g, wide):
         pl.semaphore_signal(barrier, inc=1, device_id=w, device_id_type=pl.DeviceIdType.MESH)
 
 
-def met(g):
-    pl.semaphore_wait(pltpu.get_barrier_semaphore(), 2 + g.Z)
+def met(g, wide=False):
+    pl.semaphore_wait(pltpu.get_barrier_semaphore(), len(partners(g, wide)))
 
 
 def remote(src, dst, sems, i, who):
@@ -228,6 +240,42 @@
             s += self.rz[k - 1].astype(F32)
         self.write(s)
         for c in [self.cores()] + self.far() + self.near() + self.lines():
+            c.wait_send()
+
+
+class Direct:
+    def __init__(self, g, part, out, bufs, sems):
+        self.g, self.part, self.out, self.sems = g, part, out, sems
+        self.sib, self.got = bufs
+
+    @staticmethod
+    def scratch(Z, rows, cols, dtype):
+        return [pltpu.VMEM((4, Z, rows, cols), dtype), pltpu.VMEM((4 * Z - 1, rows, cols), dtype), pltpu.SemaphoreType.DMA((2, 4 * Z))]
+
+    def cores(self):
+        g = self.g
+        return remote(self.part.at[:, 1 - g.core], self.sib, self.sems, 0, g.sibling())
+
+    def sends(self):
+        g = self.g
+        return [remote(self.part.at[g.block(d, k)], self.got.at[i], self.sems, 1 + i, g.at(d, k=k)) for i, (d, k) in enumerate(others(g))]
+
+    def B_(self):
+        self.cores().start()
+
+    def O(self):
+        self.cores().wait_recv()
+        self.part[:, self.g.core] = self.part[:, self.g.core] + self.sib[...]
+        for c in self.sends():
+            c.start()
+
+    def E(self):
+        s = self.part[self.g.block()]
+        for i, c in enumerate(self.sends()):
+            c.wait_recv()
+            s += self.got[i]
+        self.out[...] = s
+        for c in [self.cores()] + self.sends():
             c.wait_send()
 
 
@@ -280,7 +328,7 @@
     return w.reshape(*like, -1, w.shape[1])
 
 
-ROWS = ("gain", "shift", "out_bias", "freq", "gain_two", "shift_two", "down_bias", "qkv_bias", "up_bias")
+VECTORS = ("attn_norm", "out_bias", "frequencies", "mlp_norm", "down_bias", "qkv_bias", "up_bias")
 
 
 def vectors(small, r, nb, nu):
@@ -306,7 +354,8 @@
     schedule = {}
     if plan:
         dp, fsdp, r, nb, nu = plan
-        wqkv, wo, up, dnT, small, *refs = refs
+        wqkv, wo, up, dnT, *refs = refs
+        small, refs = refs[:len(VECTORS)], refs[len(VECTORS):]
         qT, kT, vT, eT, linv, oT, cosT, sinT, rows, urow, wqkv_all, wo_all, chunks, *refs = refs
         n1, trig, w, bcol, fcol, small_all, local, *sems = refs
         g = Grid(dp, fsdp)
@@ -315,7 +364,6 @@
 
         def mine(src, dst):
             mines.append(pltpu.make_async_copy(src, dst, local.at[len(mines)]))
-        mine(small, small_all.at[own])
         mine(wo, wo_all.at[own])
         for i in range(GROUPS):
             for j in range(3):
@@ -324,8 +372,9 @@
             for j, src in enumerate((up, dnT)):
                 mine(src.at[:, pl.ds(f * CHUNK, CHUNK)], chunks.at[(f, *own)].at[:, pl.ds(j * CHUNK, CHUNK)])
         saves = [pltpu.make_async_copy(w.at[i], wqkv_all.at[i], local.at[len(mines) + i]) for i in range(GROUPS)]
-        wholes = [small_all, *(w.at[i] for i in range(GROUPS)), wo_all, *(chunks.at[f] for f in range(FIRST))]
-        s, *rest = [Gather(g, a, b) for a, b in zip(wholes, sems)]
+        wholes = [small_all, *(w.at[0, :, :, :, :, pl.ds(js[0] * GW, len(js) * GW)] for js in ENDS), *(w.at[i] for i in range(1, GROUPS)), wo_all,
+                  *(chunks.at[f] for f in range(FIRST))]
+        s, qa, *rest = [Gather(g, a, b) for a, b in zip(wholes, sems)]
         q, o, c = rest[:GROUPS], rest[GROUPS], rest[GROUPS + 1:]
 
         def ready(a, b):
@@ -336,15 +385,17 @@
             for m in mines:
                 m.start()
             greet(g)
+            wide = [jnp.concatenate([x[...].astype(F32), jnp.zeros((x.shape[0], LANES - x.shape[1]), F32)], axis=1) for x in small]
+            small_all[own] = jnp.concatenate(wide + [jnp.zeros((7, LANES), F32)], axis=0).astype(BF16)
 
         def then():
-            ready(0, 1)
-            ready(2, 5)
+            ready(1, 4)
             met(g)
             s.L()
+            qa.L()
             q[0].L()
-            ready(5, 2 + 3 * GROUPS)
-            for call in (s.N, q[0].N, q[1].L, s.F, q[0].F, s.T, q[0].T, q[1].N, q[2].L, s.E, q[0].E, saves[0].start):
+            ready(4, 1 + 3 * GROUPS)
+            for call in (s.N, qa.N, q[0].N, q[1].L, s.F, qa.F, q[0].F, s.T, qa.T, q[0].T, q[1].N, q[2].L, s.E, qa.E, q[0].E, saves[0].start):
                 call()
             sm = small_all[...].astype(F32).reshape(-1, 16, LANES)
             vec, qkv, upb = vectors(sm, r, nb, nu)
@@ -353,11 +404,11 @@
             bcol[...] = qkv.T[:, 7:8]
             fcol[...] = vec.T[:, 3:4]
 
-        chunk = lambda f: functools.partial(ready, 2 + 3 * GROUPS + 2 * f, 4 + 3 * GROUPS + 2 * f)
+        chunk = lambda f: functools.partial(ready, 1 + 3 * GROUPS + 2 * f, 3 + 3 * GROUPS + 2 * f)
         schedule = {
             0: [chunk(0), c[0].L],
             1: [chunk(2), c[2].L, q[2].N],
-            2: [q[1].F, chunk(1), c[1].L, c[0].N, functools.partial(ready, 1, 2), o.L],
+            2: [q[1].F, chunk(1), c[1].L, c[0].N, functools.partial(ready, 0, 1), o.L],
             3: [q[2].F, q[1].T],
             4: [q[1].E, saves[1].start, c[2].N],
             5: [c[1].N],
@@ -465,17 +516,17 @@
     plan, params = None, {}
     if hand:
         dp, fsdp = mesh.shape["dp"], mesh.shape["fsdp"]
-        wqkv, wo, up, dnT, small = args
+        wqkv, wo, up, dnT, *small = args
         r = wqkv.shape[0]
         nb, nu = wqkv.shape[1] // d, up.shape[1] // d
         plan = dp, fsdp, r, nb, nu
-        in_specs = [ANY] * 5
+        in_specs = [ANY] * 4 + [fixed(x.shape) for x in small]
         specs += [fixed((8, d)), fixed((8, up.shape[1])), ANY, ANY, ANY]
         n = dp // 2, 2, fsdp
         shapes += [SD((8, d), F32), SD((8, up.shape[1]), F32), SD((GROUPS, *n, r, 3 * GW), BF16), SD((*n, r, d), BF16), SD((FIRST, *n, r, 2 * CHUNK), BF16)]
         scratch += [pltpu.VMEM((GROUPS, *n, r, 3 * GW), BF16), pltpu.VMEM((nb * d, 1), F32), pltpu.VMEM((d, 1), F32), pltpu.VMEM((*n, 16, LANES), BF16),
-                    pltpu.SemaphoreType.DMA((2 + 4 * GROUPS + 2 * FIRST,))]
-        scratch += Gather.scratch(fsdp) * (2 + GROUPS + FIRST)
+                    pltpu.SemaphoreType.DMA((1 + 4 * GROUPS + 2 * FIRST,))]
+        scratch += Gather.scratch(fsdp) * (3 + GROUPS + FIRST)
         params = dict(collective_id=0, has_side_effects=True)
     else:
         w, rows, bcol, fcol = args
@@ -526,24 +577,27 @@
             loads[0].wait()
         schedule = {
             0: [c[4].L],
-            4: [loads[1].wait, c[3].N, c[5].L],
-            5: [rs[0].B_, c[4].N],
-            7: [rs[0].F],
-            8: [loads[2].wait, c[3].F],
-            9: [rs[1].B_, c[4].F, c[5].N],
-            10: [c[3].T, rs[1].F, rs[0].N],
-            11: [c[4].T],
-            12: [c[3].E, rs[2].B_],
-            13: [c[4].E, rs[2].F],
-            14: [c[5].F],
-            16: [rs[1].N, rs[0].O, outs[0].start],
-            17: [c[5].T, rs[2].N],
-            19: [c[5].E],
-            20: [rs[1].O, outs[1].start],
-            21: [rs[2].O],
-            22: [rs[0].E],
+            2: [c[5].L],
+            4: [loads[1].wait, rs[0].B_, c[3].N],
+            5: [c[4].N],
+            6: [rs[0].F],
+            7: [c[3].F],
+            8: [loads[2].wait, rs[1].B_, c[5].N],
+            9: [rs[1].F],
+            10: [c[3].T, c[4].F],
+            12: [c[3].E, rs[2].B_, c[5].F],
+            13: [c[4].T, rs[2].F, rs[0].N],
+            14: [c[5].T],
+            15: [rs[1].N],
+            16: [c[4].E, rs[3].B_],
+            17: [rs[0].O, rs[3].F],
+            18: [rs[2].N],
+            19: [rs[1].O],
+            20: [c[5].E, rs[3].N, outs[0].start],
+            21: [rs[2].O, rs[0].E],
+            23: [rs[3].O, rs[1].E],
         }
-        finish = [outs[2].start], [rs[2].E, rs[1].E, *(x.wait for x in outs)]
+        finish = [outs[1].start], [rs[2].E, rs[3].E, *(x.wait for x in outs)]
         weight = lambda: w[f]
     else:
         w, out, mgrad, small, dub, dwo, dw, n2, act, hg, oacc, dacc = refs
@@ -694,40 +748,42 @@
         x = [unit(px.at[i], into(gl, i)) for i in range(count)]
         o = unit(po, into(go))
 
-        def quads(i):
+        def quads(i, js):
             def write(s):
-                for j in range(3):
-                    gqkv[:, (j * GROUPS + i) * GW:(j * GROUPS + i + 1) * GW] = s[:, j * GW:(j + 1) * GW]
+                for j in js:
+                    gqkv[:, (j * GROUPS + i) * GW:(j * GROUPS + i + 1) * GW] = s[:, (j - js[0]) * GW:(j - js[0] + 1) * GW]
             return write
-        q = [unit(pq.at[i], quads(i)) for i in range(GROUPS)]
-        sm = unit(ps, into(gs))
+        q = [unit(pq.at[i], quads(i, (0, 1, 2))) for i in range(GROUPS - 1)]
+        q += [unit(pq.at[GROUPS - 1, :, :, :, :, pl.ds(js[0] * GW, len(js) * GW)], quads(GROUPS - 1, js)) for js in ENDS]
+        sm = Direct(g, ps, gs, refs[:2], refs[2])
 
         def begin():
             for m in loads:
                 m.start()
-            greet(g)
+            greet(g, True)
 
         def then():
-            met(g)
+            met(g, True)
             loads[-1].wait()
             o.B_()
 
         schedule = {
-            1: [loads[0].wait, x[0].B_, loads[1].wait, x[1].B_],
-            3: [o.F, x[0].F, loads[2].wait, x[2].B_],
-            4: [x[1].F],
-            5: [x[2].F, o.N],
-            6: [q[0].B_, x[0].N],
-            7: [x[2].N, q[0].F],
-            9: [x[0].O, x[1].N],
+            0: [loads[0].wait, x[0].B_],
+            2: [loads[1].wait, x[1].B_],
+            3: [x[0].F, o.F],
+            6: [q[0].B_],
+            7: [x[0].N],
+            8: [q[0].F, o.N],
+            9: [x[1].F],
             12: [q[1].B_, o.O],
-            13: [q[1].F, x[2].O, x[1].O, q[0].N],
-            14: [q[1].N],
-            15: [q[0].O],
-            16: [x[0].E, q[1].O, x[2].E],
-            17: [o.E],
+            13: [x[1].N],
+            14: [q[1].F],
+            15: [q[0].N, x[0].O],
+            16: [q[1].N],
+            17: [x[1].O, q[0].O],
         }
-        tail = [[q[2].B_], [sm.B_, q[2].F, sm.F, q[0].E, x[1].E, q[2].N, sm.N, q[1].E, q[2].O, sm.O, q[2].E, sm.E]]
+        tail = [[q[2].B_, q[3].B_], [q[2].F, q[3].F, q[1].O, o.E],
+                [sm.B_, q[2].N, q[3].N, x[0].E, sm.O, x[1].E, q[0].E, q[1].E, q[2].O, q[3].O, sm.E, q[2].E, q[3].E]]
         weight = lambda: flat(w[0])
     else:
         tgrad, dwqkv, vec, qb, n1, dacc, mg = refs
@@ -805,34 +861,40 @@
             for call in tail[0]:
                 call()
 
-    dn = dot(m, weight(), 0, 1)
+    def gradient(i):
+        return dot(mg[i], weight(), 0, 1)
 
     @pl.when(quad == 0)
     def _():
-        dacc[slot] = dn
-
-    @pl.when(quad > 0)
+        dacc[slot] = gradient(slot)
+
+    @pl.when((quad > 0) & (quad < lastq))
     def _():
-        dacc[slot] += dn
-
-    @pl.when(quad == lastq)
+        dacc[slot] += gradient(slot)
+
+    @pl.when((quad == lastq) & (slot == lasts))
     def _():
-        xhat, rstd = stats(tok[slot].astype(F32))
-        dn = dacc[slot]
-        tgrad[slot] = (mgrad[slot] + ln_back(dn, rows[0:1, :], xhat, rstd)).astype(BF16)
-        vec[0:1, :] += jnp.sum(dn * xhat, axis=0, keepdims=True)
-        vec[1:2, :] += jnp.sum(dn, axis=0, keepdims=True)
-
-    if plan:
-        @pl.when((quad == lastq) & (slot == lasts))
-        def _():
+        def end(i, carry):
+            xhat, rstd = stats(tok[i].astype(F32))
+            dn = dacc[i] + gradient(i)
+            tgrad[i] = (mgrad[i] + ln_back(dn, rows[0:1, :], xhat, rstd)).astype(BF16)
+            vec[0:1, :] += jnp.sum(dn * xhat, axis=0, keepdims=True)
+            vec[1:2, :] += jnp.sum(dn, axis=0, keepdims=True)
+
+            @pl.when(i == 0)
+            def _():
+                for call in tail[1]:
+                    call()
+            return carry
+        lax.fori_loop(0, tok.shape[0], end, 0)
+        if plan:
             cs, zs = ps.shape[1:3]
 
             def store(i, x):
                 ps[i // (cs * zs), i // zs % cs, i % zs] = x
             spread(vec[...], qb[0:1, :], dub[...], dp * fsdp, store)
-            for call in tail[1]:
-                call()
+        for call in tail[2]:
+            call()
 
 
 def attn_bwd(mesh, sides, tok, mgrad, w, wo, rows, saved, args, hand):
@@ -855,10 +917,10 @@
         outs = [(r, 3 * d), (r, d), (16, LANES), (late.shape[0], *late.shape[4:])]
         specs += [fixed(s) for s in outs]
         shapes += [SD(s, F32) for s in outs]
-        parts = [*[late.shape[1:]] * late.shape[0], dwo.shape, *[(*n, r, 3 * GW)] * GROUPS]
+        parts = [*[late.shape[1:]] * late.shape[0], dwo.shape, *[(*n, r, 3 * GW)] * (GROUPS - 1), *[(*n, r, len(js) * GW) for js in ENDS]]
         scratch += [pltpu.VMEM(vec, F32), pltpu.VMEM(qb, F32), pltpu.VMEM(late.shape, BF16), pltpu.VMEM(dwo.shape, BF16),
                     pltpu.VMEM((GROUPS, *n, r, 3 * GW), BF16), pltpu.VMEM((*n, 16, LANES), F32), pltpu.SemaphoreType.DMA((late.shape[0] + 1,))]
-        scratch += [y for s in parts for y in Scatter.scratch(fsdp, s[3], s[4], BF16)] + Scatter.scratch(fsdp, 16, LANES, F32)
+        scratch += [y for s in parts for y in Scatter.scratch(fsdp, s[3], s[4], BF16)] + Direct.scratch(fsdp, 16, LANES, F32)
         params = dict(collective_id=2, has_side_effects=True)
     else:
         in_specs = []
@@ -919,20 +981,17 @@
     count = ff // CHUNK
     hand = mesh.shape["dp"] == 8 and r % 8 == 0 and count == 6
     dnT = down.T
-    small, at = jnp.zeros((16, LANES), BF16), 0
-    for x in (attn_norm, bo, freq, mlp_norm, db, bqkv, ub):
-        x = x.reshape(-1, x.shape[-1])
-        small += jnp.pad(x, ((at, 16 - at - x.shape[0]), (0, LANES - x.shape[1])))
-        at += x.shape[0]
+    small = [x.reshape(-1, x.shape[-1]) for x in (attn_norm, bo, freq, mlp_norm, db, bqkv, ub)]
     t3 = tok.reshape(slots, t, d)
     if hand:
-        *saved, rows, urow, wqkv, wo, chunks = attn_fwd(mesh, sides, t3, (wqkv, wo, up, dnT, small), True)
+        *saved, rows, urow, wqkv, wo, chunks = attn_fwd(mesh, sides, t3, (wqkv, wo, up, dnT, *small), True)
         out, mgrad, small2, dub, dwo, late, early = mlp(mesh, tok, saved[5], wo, g, rows, urow, (chunks, up, dnT), True)
         tg, gqkv, go, gs, gl = attn_bwd(mesh, sides, t3, mgrad.reshape(t3.shape), wqkv, wo.reshape(d, d), rows, saved, (small2, dub, dwo, late), True)
         return (out, tg.reshape(-1, d)) + lay_out(gqkv, go, gs, early, gl, nb * r, nu * r)
     else:
         whole = lambda x: lax.all_gather(x, BOTH, axis=0, tiled=True)
         wqkv, wo, up, dnT = (whole(x) for x in (wqkv, wo, up, dnT))
+        small = jnp.concatenate([jnp.pad(x, ((0, 0), (0, LANES - x.shape[1]))) for x in small] + [jnp.zeros((7, LANES), BF16)], axis=0)
         small = lax.all_gather(small, BOTH, axis=0).astype(F32)
         wide = lambda i, k: small[:, i, :k * r].reshape(1, k * d)
         rows = small[:, :8, :r].transpose(1, 0, 2).reshape(8, d)

time: 215 us -> 209 us (0.972)
  Pallas kernels: 210 us -> 205 us
    pallas_call x1, Pallas kernels: 75.2 us -> 68.3 us  [attn_bwd(): pl.pallas_call(functools.partial(attn_bwd_kernel, plan), grid=(GROUPS, sl...]
    pallas_call x1, Pallas kernels: 67.4 us -> 71 us  [mlp(): pl.pallas_call(functools.partial(mlp_kernel, plan), grid=(count,), in_spe...]
where the time goes in v2:
time: 209 us
  Pallas kernels  205 us (98%)
  local copies, waits for them, and re-layouts  3.4 us (2%)
    pallas_call x1, Pallas kernels, mlp(): pl.pallas_call(functools.partial(mlp_kernel, plan), grid=(count,), in_spe...  71 us
    pallas_call x1, Pallas kernels, attn_bwd(): pl.pallas_call(functools.partial(attn_bwd_kernel, plan), grid=(GROUPS, sl...  68.3 us
    pallas_call x1, Pallas kernels, attn_fwd(): pl.pallas_call(functools.partial(attn_fwd_kernel, plan), grid=(GROUPS, sl...  63.7 us

profile of v2, /device:TPU:0, one launch (start us, length us, event | category | flops | bytes accessed | tf_op | source)
XLA Modules:
  0.0 209.2 jit_solution(9183802552265447)
XLA Ops:
  0.6 63.7 %attn_fwd.1 = (bf16[2,768,600]{2,1,0:T(8,128)(2,1)}, bf16[2,768,600]{2,1,0:T(8,128)(2,1)}, bf16[2,768,600]{2,1,0:T(8,128)(2,1)}, bf16[24,600,600]{2,1,0:T(8,128)...) custom-call(s32[2,3]{1,0:T(2,128)} %refs_0_.5, ...), custom_call_target="tpu_custom_call" | custom-call | tf_op jit(solution)/shard_map/attn_fwd/pallas_call | solution.py:534
  64.3 71.0 %mlp.1 = (bf16[1200,768]{1,0:T(8,128)(2,1)}, f32[1200,768]{1,0:T(8,128)}, f32[8,768]{1,0:T(8,128)}, f32[1,3072]{1,0:T(1,128)}, bf16[4,2,4,24,768]{4,3,2,1,0:T(8,...) custom-call(bf16[1200,768]{1,0:T(8,128)(2,1)} %refs_0_.4, ...), custom_call_target="tpu_custom_call" | custom-call | tf_op jit(solution)/shard_map/mlp/pallas_call | solution.py:709
  135.3 0.0 copy-start
  135.3 68.3 %attn_bwd.1 = (bf16[2,600,768]{2,1,0:T(8,128)(2,1)}, f32[24,2304]{1,0:T(8,128)}, f32[24,768]{1,0:T(8,128)}, f32[16,128]{1,0:T(8,128)}, f32[2,24,1024]{2,1,0:T(8,128)}) custom-call(s32[2,3]{1,0:T(2,128)} %refs_0_.5, bf16[2,600,768]{2,1,0:T(8,128)(2,1)} %bitcast.17, f32[2,600,768]{2,1,0:T(8,128)} %bitcast.19, ...), custom_call_target="tpu_custom_call" | custom-call | tf_op jit(solution)/shard_map/attn_bwd/pallas_call | solution.py:929
  203.6 2.1 %lay_out.1 = (f32[2,24]{1,0:T(2,128)}, f32[24,2304]{1,0:T(8,128)}, f32[1,72]{1,0:T(1,128)}, f32[24,768]{1,0:T(8,128)}, f32[1,24]{1,0:T(1,128)}, /*index=5*/f32[1...) custom-call(f32[24,2304]{1,0:T(8,128)} %get-tuple-element.69.gqkv, ...), custom_call_target="tpu_custom_call" | custom-call | tf_op jit(solution)/shard_map/lay_out/pallas_call | solution.py:964
  205.8 0.0 copy-start.1
  205.8 0.0 copy-done
  205.8 1.2 copy.29
  207.0 0.9 copy-done.1
  207.9 1.2 copy.30
Async XLA Ops:
  135.3 70.5 %copy-start = (bf16[1200,768]{1,0:T(8,128)(2,1)S(1)}, bf16[1200,768]{1,0:T(8,128)(2,1)}, u32[]{:S(2)}) copy-start(bf16[1200,768]{1,0:T(8,128)(2,1)} %get-tuple-element.98) | copy-start | bytes 5529604
  205.8 2.2 %copy-start.1 = (bf16[2,600,768]{2,1,0:T(8,128)(2,1)S(1)}, bf16[2,600,768]{2,1,0:T(8,128)(2,1)}, u32[]{:S(2)}) copy-start(bf16[2,600,768]{2,1,0:T(8,128)(2,1)} %get-tuple-element.68) | copy-start | bytes 5529604

commit v3 on v2

--- a/solution.py
+++ b/solution.py
@@ -395,7 +395,7 @@
             qa.L()
             q[0].L()
             ready(4, 1 + 3 * GROUPS)
-            for call in (s.N, qa.N, q[0].N, q[1].L, s.F, qa.F, q[0].F, s.T, qa.T, q[0].T, q[1].N, q[2].L, s.E, qa.E, q[0].E, saves[0].start):
+            for call in (s.N, qa.N, q[0].N, q[1].L, s.F, qa.F, q[0].F, s.T, qa.T, q[0].T, q[1].N, q[2].L, s.E):
                 call()
             sm = small_all[...].astype(F32).reshape(-1, 16, LANES)
             vec, qkv, upb = vectors(sm, r, nb, nu)
@@ -403,6 +403,10 @@
             urow[...] = upb
             bcol[...] = qkv.T[:, 7:8]
             fcol[...] = vec.T[:, 3:4]
+
+        def last():
+            for call in (qa.E, q[0].E, saves[0].start):
+                call()
 
         chunk = lambda f: functools.partial(ready, 1 + 3 * GROUPS + 2 * f, 3 + 3 * GROUPS + 2 * f)
         schedule = {
@@ -436,6 +440,8 @@
             then()
         for i in range(tok.shape[0]):
             n1[i] = n1[i] * rows[0:1, :] + rows[1:2, :]
+        if plan:
+            last()
 
     talk(schedule, step, 0, 2)
     seg, height, across = places(sides, slot, t)

time: 209 us -> 208 us (level)
  no operation moved by 1% of the time
where the time goes in v3:
time: 208 us
  Pallas kernels  204 us (98%)
  local copies, waits for them, and re-layouts  3.4 us (2%)
    pallas_call x1, Pallas kernels, mlp(): pl.pallas_call(functools.partial(mlp_kernel, plan), grid=(count,), in_spe...  71.1 us
    pallas_call x1, Pallas kernels, attn_bwd(): pl.pallas_call(functools.partial(attn_bwd_kernel, plan), grid=(GROUPS, sl...  68.2 us
    pallas_call x1, Pallas kernels, attn_fwd(): pl.pallas_call(functools.partial(attn_fwd_kernel, plan), grid=(GROUPS, sl...  62.5 us

profile of v3, /device:TPU:0, one launch (start us, length us, event | category | flops | bytes accessed | tf_op | source)
XLA Modules:
  0.0 208.1 jit_solution(14654750160005301861)
XLA Ops:
  0.6 62.5 %attn_fwd.1 = (bf16[2,768,600]{2,1,0:T(8,128)(2,1)}, bf16[2,768,600]{2,1,0:T(8,128)(2,1)}, bf16[2,768,600]{2,1,0:T(8,128)(2,1)}, bf16[24,600,600]{2,1,0:T(8,128)...) custom-call(s32[2,3]{1,0:T(2,128)} %refs_0_.5, ...), custom_call_target="tpu_custom_call" | custom-call | tf_op jit(solution)/shard_map/attn_fwd/pallas_call | solution.py:540
  63.2 71.1 %mlp.1 = (bf16[1200,768]{1,0:T(8,128)(2,1)}, f32[1200,768]{1,0:T(8,128)}, f32[8,768]{1,0:T(8,128)}, f32[1,3072]{1,0:T(1,128)}, bf16[4,2,4,24,768]{4,3,2,1,0:T(8,...) custom-call(bf16[1200,768]{1,0:T(8,128)(2,1)} %refs_0_.4, ...), custom_call_target="tpu_custom_call" | custom-call | tf_op jit(solution)/shard_map/mlp/pallas_call | solution.py:715
  134.4 0.0 copy-start
  134.4 68.2 %attn_bwd.1 = (bf16[2,600,768]{2,1,0:T(8,128)(2,1)}, f32[24,2304]{1,0:T(8,128)}, f32[24,768]{1,0:T(8,128)}, f32[16,128]{1,0:T(8,128)}, f32[2,24,1024]{2,1,0:T(8,128)}) custom-call(s32[2,3]{1,0:T(2,128)} %refs_0_.5, bf16[2,600,768]{2,1,0:T(8,128)(2,1)} %bitcast.17, f32[2,600,768]{2,1,0:T(8,128)} %bitcast.19, ...), custom_call_target="tpu_custom_call" | custom-call | tf_op jit(solution)/shard_map/attn_bwd/pallas_call | solution.py:935
  202.6 2.1 %lay_out.1 = (f32[2,24]{1,0:T(2,128)}, f32[24,2304]{1,0:T(8,128)}, f32[1,72]{1,0:T(1,128)}, f32[24,768]{1,0:T(8,128)}, f32[1,24]{1,0:T(1,128)}, /*index=5*/f32[1...) custom-call(f32[24,2304]{1,0:T(8,128)} %get-tuple-element.69.gqkv, ...), custom_call_target="tpu_custom_call" | custom-call | tf_op jit(solution)/shard_map/lay_out/pallas_call | solution.py:970
  204.7 0.0 copy-start.1
  204.7 0.0 copy-done
  204.7 1.2 copy.29
  205.9 0.9 copy-done.1
  206.9 1.2 copy.30
Async XLA Ops:
  134.4 70.4 %copy-start = (bf16[1200,768]{1,0:T(8,128)(2,1)S(1)}, bf16[1200,768]{1,0:T(8,128)(2,1)}, u32[]{:S(2)}) copy-start(bf16[1200,768]{1,0:T(8,128)(2,1)} %get-tuple-element.98) | copy-start | bytes 5529604
  204.7 2.2 %copy-start.1 = (bf16[2,600,768]{2,1,0:T(8,128)(2,1)S(1)}, bf16[2,600,768]{2,1,0:T(8,128)(2,1)}, u32[]{:S(2)}) copy-start(bf16[2,600,768]{2,1,0:T(8,128)(2,1)} %get-tuple-element.68) | copy-start | bytes 5529604
